TPU v7x, 128 devices: a whole 4x4x4 slice. The times are simulated.
128 devices in a mesh: seq: 64 (over y, x, z), head: 2 (over core).
Axes of the slice: x: 4, y: 4, z: 4, core: 2. Of those that a mesh axis runs over, the one named last changes fastest.
Arguments:
- queries: bfloat16 [8192, 80, 576], P('seq', 'head'), may hold values from -117 to 117
- latent: bfloat16 [8192, 576], P('seq'), may hold values from -6 to 6
- d_out: bfloat16 [8192, 80, 512], P('seq', 'head'), may hold values from -6 to 6
- index_q: bfloat16 [8192, 64, 128], P('seq', 'head'), may hold values from -8 to 8
- index_w: bfloat16 [8192, 64], P('seq', 'head'), may hold values from -4 to 4
- index_k: bfloat16 [8192, 128], P('seq'), may hold values from -6 to 6
- picks: int32 [8192, 4], P('seq'), may hold values from -1 to 63, as said below
Outputs:
- d_queries: bfloat16 [8192, 80, 576], P('seq', 'head')
- d_latent: bfloat16 [8192, 576], P('seq')
- d_index_q: bfloat16 [8192, 64, 128], P('seq', 'head')
- d_index_w: float32 [8192, 64], P('seq', 'head')
- d_index_k: bfloat16 [8192, 128], P('seq')
Inputs may be any that keep to these rules, and one draw needn't show every extreme that they name: `picks`: row t lists first its own block b = t // 128, then block 0 if b > 0, then 4 - 2 further distinct blocks among 1 to b - 1; slots without a block hold -1, so a row lists min(4, b + 1) distinct blocks.
All inputs are finite; a program needn't handle non-finite values.
Results may differ from a plain program's by a relative error of at most 0.038.
Values may be sent and summed in bfloat16 or wider, within the bound.
No kernel may reach another device: no remote copies, remote signals or barrier semaphores. Data moves between devices by JAX's collectives and lax.ppermute only.
A program may use at most 256 MiB of HBM per device.

v0:
```python
import math

import jax
import jax.numpy as jnp
from jax import lax
from jax.sharding import PartitionSpec as P

BLOCK = 128
PICK = 4
H = 80
IH = 64


softmax_scale = 192.0 ** (-0.5)
kl_weight = 32.0
neg_large = -1e30


def masked_softmax(scores, allowed):
    masked = jnp.where(allowed, scores, neg_large)
    top = jnp.max(masked, axis=-1, keepdims=True)
    expo = jnp.where(allowed, jnp.exp(masked - top), 0.0)
    return expo / jnp.sum(expo, axis=-1, keepdims=True)


def per_device(queries, latent, d_out, index_q, index_w, index_k, picks):
    rows, heads, width = queries.shape
    vwidth = d_out.shape[2]
    iwidth = index_k.shape[1]
    group = math.gcd(BLOCK, 32)
    ngroups = rows // group
    span = PICK * BLOCK
    shared_span = 2 * BLOCK
    inv_root = IH ** (-0.5)
    all_lat, all_ik = (
        lax.all_gather(latent, "seq", axis=0, tiled=True),
        lax.all_gather(index_k, "seq", axis=0, tiled=True),
    )
    nblk = all_lat.shape[0] // BLOCK
    lat_blocks = all_lat.reshape(nblk, BLOCK, width)
    ik_blocks = all_ik.reshape(nblk, BLOCK, iwidth)
    offsets = jnp.arange(BLOCK, dtype=jnp.int32)
    base_pos = lax.axis_index("seq") * rows
    padded_out = jnp.pad(d_out, ((0, 0), (0, 0), (0, width - vwidth)))
    stacked_all = jnp.concatenate([queries, padded_out], axis=1)

    def context(stepno):
        first = stepno * group
        qpos = base_pos + first + jnp.arange(group, dtype=jnp.int32)
        own = qpos[0] // BLOCK
        chosen = lax.dynamic_slice_in_dim(picks, first, group, 0)
        blk = jnp.maximum(chosen, 0)
        kpos = (blk[:, :, None] * BLOCK + offsets).reshape(group, span)
        allowed = jnp.repeat(chosen >= 0, BLOCK, axis=1) & (kpos <= qpos[:, None])
        return (first, own, blk[:, 2:], allowed)

    def shared_rows(blocks_all, own):
        return jnp.concatenate(
            [lax.dynamic_index_in_dim(blocks_all, own, 0, keepdims=False), blocks_all[0]], axis=0
        )

    def index_gate(first, own, extra_blk):
        iq_grp = lax.dynamic_slice_in_dim(index_q, first, group, 0)
        ik_shared = shared_rows(ik_blocks, own)
        ik_extra = ik_blocks[extra_blk].reshape(group, -1, iwidth)
        gate = jnp.concatenate(
            [
                jnp.einsum("tjd,sd->tjs", iq_grp, ik_shared, preferred_element_type=jnp.float32),
                jnp.einsum("tjd,tsd->tjs", iq_grp, ik_extra, preferred_element_type=jnp.float32),
            ],
            axis=2,
        )
        return (iq_grp, ik_shared, ik_extra, gate)

    def index_partial(stepno):
        first, own, extra_blk, allowed = context(stepno)
        iq_grp, ik_shared, ik_extra, gate = index_gate(first, own, extra_blk)
        weights = lax.dynamic_slice_in_dim(index_w, first, group, 0).astype(jnp.float32)
        return jnp.sum(weights[:, :, None] * jax.nn.softplus(gate), axis=1) * inv_root

    def attend(acc_lat, stepno):
        first, own, extra_blk, allowed = context(stepno)
        stacked = lax.dynamic_slice_in_dim(stacked_all, first, group, 0)
        lat_shared = shared_rows(lat_blocks, own)
        lat_extra = lat_blocks[extra_blk].reshape(group, -1, width)
        both = jnp.concatenate(
            [
                jnp.einsum("thd,sd->ths", stacked, lat_shared, preferred_element_type=jnp.float32),
                jnp.einsum("thd,tsd->ths", stacked, lat_extra, preferred_element_type=jnp.float32),
            ],
            axis=2,
        )
        scores = both[:, :heads] * softmax_scale
        dprob = both[:, heads:]
        probs = masked_softmax(scores, allowed[:, None, :])
        delta = jnp.sum(probs * dprob, axis=2, keepdims=True)
        dscore = (probs * (dprob - delta) * softmax_scale).astype(jnp.bfloat16)
        grads = jnp.concatenate([dscore, probs.astype(jnp.bfloat16)], axis=1)
        d_q = (
            jnp.einsum(
                "ths,sd->thd",
                dscore[:, :, :shared_span],
                lat_shared,
                preferred_element_type=jnp.float32,
            )
            + jnp.einsum(
                "ths,tsd->thd",
                dscore[:, :, shared_span:],
                lat_extra,
                preferred_element_type=jnp.float32,
            )
        ).astype(jnp.bfloat16)
        upd_shared = jnp.einsum(
            "ths,thd->sd", grads[:, :, :shared_span], stacked, preferred_element_type=jnp.float32
        )
        upd_extra = jnp.einsum(
            "ths,thd->tsd", grads[:, :, shared_span:], stacked, preferred_element_type=jnp.float32
        )
        acc_lat = acc_lat.at[own].add(upd_shared[:BLOCK])
        acc_lat = acc_lat.at[0].add(upd_shared[BLOCK:])
        acc_lat = acc_lat.at[extra_blk].add(upd_extra.reshape(group, PICK - 2, BLOCK, width))
        return (acc_lat, (d_q, jnp.sum(probs, axis=1)))

    steps_all = jnp.arange(ngroups, dtype=jnp.int32)
    lat_start = jnp.zeros((nblk, BLOCK, width), jnp.float32)

    def attend_both(acc_lat, stepno):
        acc_lat, outs = attend(acc_lat, stepno)
        return (acc_lat, (outs[0], outs[1], index_partial(stepno)))

    acc_lat, (d_q, target_part, logit_part) = lax.scan(attend_both, lat_start, steps_all)
    target, logits = lax.psum((target_part, logit_part), "head")

    def index_back(acc_ik, inputs):
        stepno, logit_grp, target_grp = inputs
        first, own, extra_blk, allowed = context(stepno)
        iq_grp, ik_shared, ik_extra, gate = index_gate(first, own, extra_blk)
        weights = lax.dynamic_slice_in_dim(index_w, first, group, 0).astype(jnp.float32)
        soft = masked_softmax(logit_grp, allowed)
        d_logit = jnp.where(allowed, kl_weight * (soft - target_grp / H), 0.0)
        d_w = jnp.sum(d_logit[:, None, :] * jax.nn.softplus(gate), axis=2) * inv_root
        d_gate = (
            d_logit[:, None, :] * weights[:, :, None] * jax.nn.sigmoid(gate) * inv_root
        ).astype(jnp.bfloat16)
        d_iq = (
            jnp.einsum(
                "tjs,sd->tjd",
                d_gate[:, :, :shared_span],
                ik_shared,
                preferred_element_type=jnp.float32,
            )
            + jnp.einsum(
                "tjs,tsd->tjd",
                d_gate[:, :, shared_span:],
                ik_extra,
                preferred_element_type=jnp.float32,
            )
        ).astype(jnp.bfloat16)
        upd_shared = jnp.einsum(
            "tjs,tjd->sd", d_gate[:, :, :shared_span], iq_grp, preferred_element_type=jnp.float32
        )
        upd_extra = jnp.einsum(
            "tjs,tjd->tsd", d_gate[:, :, shared_span:], iq_grp, preferred_element_type=jnp.float32
        )
        acc_ik = acc_ik.at[own].add(upd_shared[:BLOCK])
        acc_ik = acc_ik.at[0].add(upd_shared[BLOCK:])
        acc_ik = acc_ik.at[extra_blk].add(upd_extra.reshape(group, PICK - 2, BLOCK, iwidth))
        return (acc_ik, (d_iq, d_w))

    ik_start = jnp.zeros((nblk, BLOCK, iwidth), jnp.float32)
    acc_ik, (d_iq, d_w) = lax.scan(index_back, ik_start, (steps_all, logits, target))
    d_queries = d_q.reshape(rows, heads, width)
    d_index_q = d_iq.reshape(rows, -1, iwidth)
    d_index_w = d_w.reshape(rows, -1)
    flat_lat = acc_lat.reshape(nblk * BLOCK, width)
    flat_ik = acc_ik.reshape(nblk * BLOCK, iwidth)
    lat_sum, ik_sum = (
        lax.psum_scatter(flat_lat, "seq", scatter_dimension=0, tiled=True),
        lax.psum_scatter(flat_ik, "seq", scatter_dimension=0, tiled=True),
    )
    lat_sum, ik_sum = (
        lax.psum(lat_sum.astype(jnp.bfloat16), "head").astype(jnp.float32),
        lax.psum(ik_sum.astype(jnp.bfloat16), "head").astype(jnp.float32),
    )
    d_latent = lat_sum.astype(jnp.bfloat16)
    d_index_k = ik_sum.astype(jnp.bfloat16)
    return (d_queries, d_latent, d_index_q, d_index_w, d_index_k)


def solution(mesh):
    return jax.shard_map(
        per_device,
        mesh=mesh,
        in_specs=(
            P("seq", "head", None),
            P("seq", None),
            P("seq", "head", None),
            P("seq", "head", None),
            P("seq", "head"),
            P("seq", None),
            P("seq", None),
        ),
        out_specs=(
            P("seq", "head", None),
            P("seq", None),
            P("seq", "head", None),
            P("seq", "head"),
            P("seq", None),
        ),
        check_vma=False,
    )
```

profile of v0, /device:TPU:1, one launch (start us, length us, event | category | flops | bytes accessed | tf_op | source)
XLA Modules:
  0.0 1698.3 jit_solution(16132578952700181361)
XLA Ops:
  33.3 83.6 %all-gather.3.cloned.1.call-done = bf16[8192,576]{0,1:T(8,128)(2,1)} async-done(((bf16[128,576]{0,1:T(8,128)(2,1)}), bf16[8192,576]{0,1:T(8,128)(2,1)}) %all-gather.3.cloned.1.call-update) | async-done | bytes 9437200 | tf_op jit(solution)/shard_map/all_gather | solution.py:36
  126.8 57.9 %all-gather.5.cloned.1.call-done = bf16[8192,128]{1,0:T(8,128)(2,1)} async-done(((bf16[128,128]{1,0:T(8,128)(2,1)}), bf16[8192,128]{1,0:T(8,128)(2,1)}) %all-gather.5.cloned.1.call-update) | async-done | bytes 2097168 | tf_op jit(solution)/shard_map/all_gather | solution.py:37
  193.5 844.7 %while.41 = (s32[]{:T(128)}, f32[64,128,576]{1,2,0:T(8,128)}, bf16[4,32,40,576]{3,2,1,0:T(8,128)(2,1)}, f32[4,32,512]{2,1,0:T(8,128)}, f32[4,32,512]{2,1,0:T(8,1...) while((s32[]{:T(128)}, f32[64,128,576]{1,2,0:T(8,128)}, ...), condition=%wide.region_8.9_spmd.clone, body=%wide.region_0.8_spmd.clone.sunk | while | flops 3938612224 | bytes 379789024 | solution.py:131
  295.3 23.4 %copy.75 = f32[32,256,576]{1,0,2:T(8,128)} copy(f32[32,256,576]{1,2,0:T(8,128)S(1)} %fusion.170) | data formatting | bytes 37748736 | tf_op jit(solution)/shard_map/while/body/eval_jaxpr/ths,thd->tsd/dot_general | solution.py:116
  318.7 19.5 %reshape.597 = f32[64,128,576]{1,0,2:T(8,128)} reshape(f32[32,256,576]{1,0,2:T(8,128)} %copy.75) | data formatting | bytes 37748736 | tf_op jit(solution)/shard_map/while/body/eval_jaxpr/reshape | solution.py:121
  360.0 37.2 %scatter_fusion = f32[64,128,576]{1,2,0:T(8,128)} fusion(f32[64,128,576]{1,2,0:T(8,128)} %fusion.169, s32[64]{0:T(128)S(1)} %reshape.595, f32[64,128,576]{1,2,0:T(8,128)} %copy.76), kind=kCustom, calls=%fused_computation.3.clone.clone.1 | custom fusion | flops 4718592 | bytes 56623360 | tf_op jit(solution)/shard_map/while/body/eval_jaxpr/scatter-add | solution.py:121
  436.7 26.3 %reshape.596 = bf16[32,256,576]{1,0,2:T(8,128)(2,1)} reshape(bf16[64,128,576]{1,0,2:T(8,128)(2,1)} %copy.74) | data formatting | bytes 18874368 | tf_op jit(solution)/shard_map/while/body/eval_jaxpr/reshape | solution.py:85
  510.8 23.4 %copy.75 = f32[32,256,576]{1,0,2:T(8,128)} copy(f32[32,256,576]{1,2,0:T(8,128)S(1)} %fusion.170) | data formatting | bytes 37748736 | tf_op jit(solution)/shard_map/while/body/eval_jaxpr/ths,thd->tsd/dot_general | solution.py:116
  534.2 19.5 %reshape.597 = f32[64,128,576]{1,0,2:T(8,128)} reshape(f32[32,256,576]{1,0,2:T(8,128)} %copy.75) | data formatting | bytes 37748736 | tf_op jit(solution)/shard_map/while/body/eval_jaxpr/reshape | solution.py:121
  553.7 18.0 %copy.76 = f32[64,128,576]{1,2,0:T(8,128)} copy(f32[64,128,576]{1,0,2:T(8,128)} %reshape.597) | data formatting | bytes 37748736 | tf_op jit(solution)/shard_map/while/body/eval_jaxpr/reshape | solution.py:121
  575.7 37.2 %scatter_fusion = f32[64,128,576]{1,2,0:T(8,128)} fusion(f32[64,128,576]{1,2,0:T(8,128)} %fusion.169, s32[64]{0:T(128)S(1)} %reshape.595, f32[64,128,576]{1,2,0:T(8,128)} %copy.76), kind=kCustom, calls=%fused_computation.3.clone.clone.1 | custom fusion | flops 4718592 | bytes 56623360 | tf_op jit(solution)/shard_map/while/body/eval_jaxpr/scatter-add | solution.py:121
  714.7 23.4 %copy.75 = f32[32,256,576]{1,0,2:T(8,128)} copy(f32[32,256,576]{1,2,0:T(8,128)S(1)} %fusion.170) | data formatting | bytes 37748736 | tf_op jit(solution)/shard_map/while/body/eval_jaxpr/ths,thd->tsd/dot_general | solution.py:116
  738.2 19.5 %reshape.597 = f32[64,128,576]{1,0,2:T(8,128)} reshape(f32[32,256,576]{1,0,2:T(8,128)} %copy.75) | data formatting | bytes 37748736 | tf_op jit(solution)/shard_map/while/body/eval_jaxpr/reshape | solution.py:121
  757.7 17.8 %copy.76 = f32[64,128,576]{1,2,0:T(8,128)} copy(f32[64,128,576]{1,0,2:T(8,128)} %reshape.597) | data formatting | bytes 37748736 | tf_op jit(solution)/shard_map/while/body/eval_jaxpr/reshape | solution.py:121
  779.5 37.2 %scatter_fusion = f32[64,128,576]{1,2,0:T(8,128)} fusion(f32[64,128,576]{1,2,0:T(8,128)} %fusion.169, s32[64]{0:T(128)S(1)} %reshape.595, f32[64,128,576]{1,2,0:T(8,128)} %copy.76), kind=kCustom, calls=%fused_computation.3.clone.clone.1 | custom fusion | flops 4718592 | bytes 56623360 | tf_op jit(solution)/shard_map/while/body/eval_jaxpr/scatter-add | solution.py:121
  856.2 26.3 %reshape.596 = bf16[32,256,576]{1,0,2:T(8,128)(2,1)} reshape(bf16[64,128,576]{1,0,2:T(8,128)(2,1)} %copy.74) | data formatting | bytes 18874368 | tf_op jit(solution)/shard_map/while/body/eval_jaxpr/reshape | solution.py:85
  930.3 23.4 %copy.75 = f32[32,256,576]{1,0,2:T(8,128)} copy(f32[32,256,576]{1,2,0:T(8,128)S(1)} %fusion.170) | data formatting | bytes 37748736 | tf_op jit(solution)/shard_map/while/body/eval_jaxpr/ths,thd->tsd/dot_general | solution.py:116
  953.7 19.5 %reshape.597 = f32[64,128,576]{1,0,2:T(8,128)} reshape(f32[32,256,576]{1,0,2:T(8,128)} %copy.75) | data formatting | bytes 37748736 | tf_op jit(solution)/shard_map/while/body/eval_jaxpr/reshape | solution.py:121
  973.2 18.0 %copy.76 = f32[64,128,576]{1,2,0:T(8,128)} copy(f32[64,128,576]{1,0,2:T(8,128)} %reshape.597) | data formatting | bytes 37748736 | tf_op jit(solution)/shard_map/while/body/eval_jaxpr/reshape | solution.py:121
  995.3 37.2 %scatter_fusion = f32[64,128,576]{1,2,0:T(8,128)} fusion(f32[64,128,576]{1,2,0:T(8,128)} %fusion.169, s32[64]{0:T(128)S(1)} %reshape.595, f32[64,128,576]{1,2,0:T(8,128)} %copy.76), kind=kCustom, calls=%fused_computation.3.clone.clone.1 | custom fusion | flops 4718592 | bytes 56623360 | tf_op jit(solution)/shard_map/while/body/eval_jaxpr/scatter-add | solution.py:121
  1067.7 149.1 %while.42 = (s32[]{:T(128)}, f32[64,128,128]{2,1,0:T(8,128)}, bf16[4,32,32,128]{3,2,1,0:T(8,128)(2,1)}, f32[4,32,32]{2,1,0:T(8,128)}, s32[4]{0:T(128)S(1)}, /*in...) while((s32[]{:T(128)}, f32[64,128,128]{2,1,0:T(8,128)}, ...), condition=%wide.region_19.20_spmd.clone.clone, body=%wide.region_13.19_spmd.clone.clone.sunk | while | flops 412994112 | bytes 40766600 | solution.py:171
  1216.9 91.8 %reduce-scatter.3.cloned.1.call-done = f32[128,576]{0,1:T(8,128)} async-done(((f32[8192,576]{0,1:T(8,128)}), f32[128,576]{0,1:T(8,128)}) %reduce-scatter.3.cloned.1.call-update) | async-done | bytes 294928 | tf_op jit(solution)/shard_map/reduce_scatter | solution.py:178
  1321.7 297.4 %reduce-scatter.5.cloned.1.call-done = f32[128,128]{1,0:T(8,128)} async-done(((f32[8192,128]{1,0:T(8,128)}), f32[128,128]{1,0:T(8,128)}) %reduce-scatter.5.cloned.1.call-update) | async-done | bytes 65552 | tf_op jit(solution)/shard_map/reduce_scatter | solution.py:179
  1620.0 53.3 %psum.31 = bf16[128,128]{1,0:T(8,128)(2,1)} all-reduce(bf16[128,128]{1,0:T(8,128)(2,1)S(1)} %convert_element_type.55), channel_id=1, replica_groups=mesh['seq'=64,'head'=2] {'head'}, use_global_device_ids=true, to_apply=%region_21.22 | all-reduce | flops 16384 | bytes 65536 | tf_op jit(solution)/shard_map/psum | solution.py:183
  (395 shorter events, 658.6 us)
Async XLA Ops:
  7.2 109.7 %all-gather.3.cloned.1.call-start = ((), (), s32[]{:S(2)}) async-start(), calls=%async_computation.2 | async-start | bytes 9584640 | tf_op jit(solution)/shard_map/all_gather | solution.py:36
  7.9 176.8 %all-gather.5.cloned.1.call-start = ((), (), s32[]{:S(2)}) async-start(), calls=%async_computation.3 | async-start | bytes 2129920 | tf_op jit(solution)/shard_map/all_gather | solution.py:37
  8.6 1056.5 %all-reduce.7.cloned.1.call-start = ((), (), s32[]{:S(2)}) async-start(), calls=%async_computation.7 | async-start | bytes 1048576 | tf_op jit(solution)/shard_map/psum | solution.py:132
  208.8 48.6 %copy-start.1 = (f32[32,80,256]{2,1,0:T(8,128)}, f32[32,80,256]{2,1,0:T(8,128)S(1)}, u32[]{:S(2)}) copy-start(f32[32,80,256]{2,1,0:T(8,128)S(1)} %fusion.163) | copy-start | bytes 7864324 | tf_op jit(solution)/shard_map/while
  257.4 15.1 slice-start
  338.2 17.8 %copy-start.3 = (f32[256,576]{0,1:T(8,128)S(1)}, f32[256,576]{0,1:T(8,128)}, u32[]{:S(2)}) copy-start(f32[256,576]{0,1:T(8,128)} %fusion.167) | copy-start | bytes 1769476 | tf_op jit(solution)/shard_map/while
  360.0 37.2 %copy-start.6 = (s32[128,4]{1,0:T(8,128)S(1)}, s32[128,4]{1,0:T(8,128)}, u32[]{:S(2)}) copy-start(s32[128,4]{1,0:T(8,128)} %copy-done.5) | copy-start | bytes 6148 | tf_op jit(solution)/shard_map/while
  412.9 60.2 %copy-start.1 = (f32[32,80,256]{2,1,0:T(8,128)}, f32[32,80,256]{2,1,0:T(8,128)S(1)}, u32[]{:S(2)}) copy-start(f32[32,80,256]{2,1,0:T(8,128)S(1)} %fusion.163) | copy-start | bytes 7864324 | tf_op jit(solution)/shard_map/while
  473.1 15.1 slice-start
  553.7 18.0 %copy-start.3 = (f32[256,576]{0,1:T(8,128)S(1)}, f32[256,576]{0,1:T(8,128)}, u32[]{:S(2)}) copy-start(f32[256,576]{0,1:T(8,128)} %fusion.167) | copy-start | bytes 1769476 | tf_op jit(solution)/shard_map/while
  575.7 37.2 %copy-start.6 = (s32[128,4]{1,0:T(8,128)S(1)}, s32[128,4]{1,0:T(8,128)}, u32[]{:S(2)}) copy-start(s32[128,4]{1,0:T(8,128)} %copy-done.5) | copy-start | bytes 6148 | tf_op jit(solution)/shard_map/while
  628.5 48.6 %copy-start.1 = (f32[32,80,256]{2,1,0:T(8,128)}, f32[32,80,256]{2,1,0:T(8,128)S(1)}, u32[]{:S(2)}) copy-start(f32[32,80,256]{2,1,0:T(8,128)S(1)} %fusion.163) | copy-start | bytes 7864324 | tf_op jit(solution)/shard_map/while
  677.1 15.1 slice-start
  757.7 17.8 %copy-start.3 = (f32[256,576]{0,1:T(8,128)S(1)}, f32[256,576]{0,1:T(8,128)}, u32[]{:S(2)}) copy-start(f32[256,576]{0,1:T(8,128)} %fusion.167) | copy-start | bytes 1769476 | tf_op jit(solution)/shard_map/while
  779.5 37.2 %copy-start.6 = (s32[128,4]{1,0:T(8,128)S(1)}, s32[128,4]{1,0:T(8,128)}, u32[]{:S(2)}) copy-start(s32[128,4]{1,0:T(8,128)} %copy-done.5) | copy-start | bytes 6148 | tf_op jit(solution)/shard_map/while
  832.4 60.2 %copy-start.1 = (f32[32,80,256]{2,1,0:T(8,128)}, f32[32,80,256]{2,1,0:T(8,128)S(1)}, u32[]{:S(2)}) copy-start(f32[32,80,256]{2,1,0:T(8,128)S(1)} %fusion.163) | copy-start | bytes 7864324 | tf_op jit(solution)/shard_map/while
  892.5 15.1 slice-start
  973.2 18.0 %copy-start.3 = (f32[256,576]{0,1:T(8,128)S(1)}, f32[256,576]{0,1:T(8,128)}, u32[]{:S(2)}) copy-start(f32[256,576]{0,1:T(8,128)} %fusion.167) | copy-start | bytes 1769476 | tf_op jit(solution)/shard_map/while
  995.3 37.2 %copy-start.6 = (s32[128,4]{1,0:T(8,128)S(1)}, s32[128,4]{1,0:T(8,128)}, u32[]{:S(2)}) copy-start(s32[128,4]{1,0:T(8,128)} %copy-done.5) | copy-start | bytes 6148 | tf_op jit(solution)/shard_map/while
  1038.2 270.5 %reduce-scatter.3.cloned.1.call-start = ((), (), s32[]{:S(2)}) async-start(), calls=%async_computation.4 | async-start | bytes 19169280 | tf_op jit(solution)/shard_map/reduce_scatter | solution.py:178
  1052.7 566.4 %reduce-scatter.5.cloned.1.call-start = ((), (), s32[]{:S(2)}) async-start(), calls=%async_computation.6 | async-start | bytes 4259840 | tf_op jit(solution)/shard_map/reduce_scatter | solution.py:179
  1090.2 14.8 copy-start.8
  1164.8 14.8 copy-start.8
  1216.8 472.8 %all-reduce.5.cloned.1.call-start = ((), (), s32[]{:S(2)}) async-start(), calls=%async_computation.5 | async-start | bytes 294912 | tf_op jit(solution)/shard_map/psum | solution.py:182
  (33 other events, 205.5 us)
Sparse Core Ops, SparseCore 0:
  10.7 106.1 all-gather.2
  119.8 64.8 all-gather.4
  1038.3 26.8 all-reduce.6
  1070.5 238.1 reduce-scatter.2
  1310.9 308.1 reduce-scatter.4
  1622.1 67.4 all-reduce.4
where the time goes:
time: 1710 us; the launch traced here: 1700 us
  waiting for transfers between devices  561 us (33%)
  local copies, waits for them, and re-layouts  521 us (30%)
  other arithmetic  354 us (21%)
  matrix products  181 us (11%)
  blocking collectives  53.3 us (3%)
    reduce_scatter x1, waiting for transfers between devices, per_device(): lax.psum_scatter(flat_ik, 'seq', scatter_dimension=0, tiled=True)  297 us
    reshape x8, local copies, waits for them, and re-layouts, attend(): upd_extra.reshape(group, PICK - 2, BLOCK, width)  149 us
    scatter-add x4, other arithmetic, attend(): acc_lat.at[extra_blk].add(upd_extra.reshape(group, PICK - 2, BLOCK, width))  149 us
    gather x8, local copies, waits for them, and re-layouts, attend(): lat_extra = lat_blocks[extra_blk].reshape(group, -1, width)  95 us
    dot_general x4, local copies, waits for them, and re-layouts, attend(): jnp.einsum('ths,thd->tsd', grads[:, :, shared_span:], stacked, preferred_...  93.7 us
    reduce_scatter x1, waiting for transfers between devices, per_device(): lax.psum_scatter(flat_lat, 'seq', scatter_dimension=0, tiled=True)  91.8 us
    all_gather x1, waiting for transfers between devices, per_device(): lax.all_gather(latent, 'seq', axis=0, tiled=True)  83.6 us
    reshape x4, local copies, waits for them, and re-layouts, attend(): lat_extra = lat_blocks[extra_blk].reshape(group, -1, width)  82.2 us
  transfers between devices with their start and end apart: 6, of which 6 were waited for; matrix products, arithmetic and copies ran while one was open for 12% of the time, Pallas kernels for 0%

commit v1 on v0

v1 whole, which is shorter than its diff:
```python
import functools

import jax
import jax.numpy as jnp
from jax import lax
from jax.experimental import pallas as pl
from jax.experimental.pallas import tpu as pltpu
from jax.sharding import PartitionSpec as P

BLOCK = 128
PICK = 4
H = 80
IH = 64
LANES = 128

softmax_scale = 192.0 ** (-0.5)
kl_weight = 32.0
neg_large = -1e30
inv_root = IH ** (-0.5)

G_ATT = 8
G_IDX = 8
PAIRS = 4
HALF = BLOCK // 2
VMEM_LIMIT = 58 * 1024 * 1024


def dot(a, b, ca, cb):
    return lax.dot_general(a, b, (((ca,), (cb,)), ((), ())), preferred_element_type=jnp.float32)


def mask_row(picks_ref, t, tloc):
    lane = lax.broadcasted_iota(jnp.int32, (1, LANES), 1)
    parts = [jnp.where(lane <= tloc, 0.0, neg_large)]
    for j in range(1, PICK):
        parts.append(jnp.where(lane + picks_ref[t * PICK + j] * LANES >= 0, 0.0, neg_large))
    return jnp.concatenate(parts, axis=1)


def block_of(keys, b):
    return keys[pl.ds(2 * b, 2)].reshape(BLOCK, keys.shape[2])


def load_keys(lat_ref, keys, tails, sem):
    full = keys.shape[2] // LANES - 1
    copies = [
        pltpu.make_async_copy(
            lat_ref.at[:, pl.ds((c + 1) * HALF, HALF), :],
            keys.at[:, :, pl.ds(c * LANES, LANES)],
            sem.at[c],
        )
        for c in range(full)
    ]
    copies.append(
        pltpu.make_async_copy(
            lat_ref.at[:, pl.ds((full + 1) * HALF, HALF // 2), :], tails, sem.at[full]
        )
    )
    for cp in copies:
        cp.start()

    def finish():
        for cp in copies:
            cp.wait()

        def unpack(i, carry):
            low = tails[i]
            high = pltpu.roll(low.astype(jnp.float32), HALF, 1).astype(jnp.bfloat16)
            keys[i, :, pl.ds(full * LANES, LANES)] = jnp.concatenate([low, high], axis=0)
            return carry

        lax.fori_loop(0, keys.shape[0], unpack, 0, unroll=4)

    return finish


def attend_kernel(
    groups, heads, picks_ref, own_ref, tile_ref, pair_ref, stk_hbm, lat_ref,
    dsx_ref, dsh_ref, tgt_ref, keep_ref, send_ref,
    keys, tails, stk, extra, acc, acc_sh, sem,
):
    step = pl.program_id(0)
    own = own_ref[0]
    core = own_ref[1]
    rows = 2 * heads
    nblk = acc.shape[0]
    tokens = stk.shape[0]
    full = keys.shape[2] // LANES - 1

    @pl.when(step == 0)
    def _():
        load_stk = pltpu.make_async_copy(stk_hbm, stk, sem.at[full + 1])
        finish = load_keys(lat_ref, keys, tails, sem)
        load_stk.start()

        def zero(b, carry):
            acc[b] = jnp.zeros(acc.shape[1:], jnp.float32)
            return carry

        lax.fori_loop(0, nblk, zero, 0)
        acc_sh[...] = jnp.zeros(acc_sh.shape, jnp.float32)
        finish()
        load_stk.wait()

        def tile_pair(i, carry):
            for u in range(2):
                tile = 2 * i + u
                pairs = [pair_ref[tile * PAIRS + k] for k in range(PAIRS)]
                lhs = jnp.concatenate([stk[jnp.minimum(p // 2, tokens - 1)] for p in pairs], axis=0)
                out = dot(lhs, block_of(keys, tile_ref[1 + tile]), 1, 1)
                for k, p in enumerate(pairs):
                    extra[p] = out[k * rows : (k + 1) * rows]
            return carry

        lax.fori_loop(0, tile_ref[0], tile_pair, 0)

    ksh = jnp.concatenate([block_of(keys, own), block_of(keys, 0)], axis=0)
    stk_all = stk[pl.ds(step * groups, groups)].reshape(groups * rows, stk.shape[2])
    both_sh = dot(stk_all, ksh, 1, 1)
    ds_list, gr_list, tgt_list = [], [], []
    for g in range(groups):
        t = step * groups + g
        e0 = jnp.maximum(picks_ref[t * PICK + 2], 0)
        e1 = jnp.maximum(picks_ref[t * PICK + 3], 0)
        bias = mask_row(picks_ref, t, t)
        both_x = jnp.concatenate([extra[2 * t], extra[2 * t + 1]], axis=1)
        lo = g * rows
        scores = jnp.concatenate([both_sh[lo : lo + heads], both_x[:heads]], axis=1)
        dprob = jnp.concatenate([both_sh[lo + heads : lo + rows], both_x[heads:]], axis=1)
        scores = scores * softmax_scale + bias
        top = jnp.max(scores, axis=1, keepdims=True)
        expo = jnp.exp(scores - top)
        probs = expo * (1.0 / jnp.sum(expo, axis=1, keepdims=True))
        delta = jnp.sum(probs * dprob, axis=1, keepdims=True)
        dscore = probs * (dprob - delta) * softmax_scale
        tgt_list.append(jnp.sum(probs, axis=0, keepdims=True))
        grads = jnp.concatenate([dscore, probs], axis=0).astype(jnp.bfloat16)
        dsx_ref[2 * g] = dscore[:, 2 * BLOCK : 3 * BLOCK]
        dsx_ref[2 * g + 1] = dscore[:, 3 * BLOCK :]
        upd = dot(grads[:, 2 * BLOCK :], stk[t], 0, 0)
        acc[e0] += upd[:BLOCK]
        acc[e1] += upd[BLOCK:]
        ds_list.append(dscore[:, : 2 * BLOCK])
        gr_list.append(grads[:, : 2 * BLOCK])
    dsh_ref[...] = jnp.concatenate(ds_list, axis=0).astype(jnp.bfloat16)
    acc_sh[...] += dot(jnp.concatenate(gr_list, axis=0), stk_all, 0, 0)
    tgt_ref[...] = jnp.concatenate(tgt_list, axis=0)

    @pl.when(step == pl.num_programs(0) - 1)
    def _():
        acc[own] += acc_sh[pl.ds(0, BLOCK), :]
        acc[0] += acc_sh[pl.ds(BLOCK, BLOCK), :]

        def cast(b, carry):
            for k, which in enumerate((core, 1 - core)):
                part = acc[b, pl.ds(pl.multiple_of(which * HALF, HALF), HALF), :]
                keys[k * nblk + b] = part.astype(jnp.bfloat16)
                last = part[:, full * LANES :]
                packed = last[: HALF // 2] + pltpu.roll(last[HALF // 2 :], HALF, 1)
                tails[k * nblk + b] = packed.astype(jnp.bfloat16)
            return carry

        lax.fori_loop(0, nblk, cast, 0)
        stores = []
        for k, ref in enumerate((keep_ref, send_ref)):
            part = pl.ds(k * nblk, nblk)
            for c in range(full):
                stores.append(
                    pltpu.make_async_copy(
                        keys.at[part, :, pl.ds(c * LANES, LANES)],
                        ref.at[:, pl.ds(c * HALF, HALF), :],
                        sem.at[k * (full + 1) + c],
                    )
                )
            stores.append(
                pltpu.make_async_copy(
                    tails.at[part],
                    ref.at[:, pl.ds(full * HALF, HALF // 2), :],
                    sem.at[k * (full + 1) + full],
                )
            )
        for cp in stores:
            cp.start()
        for cp in stores:
            cp.wait()


def attend_call(picks, own, tiles, pairs, stk, gathered, heads):
    tokens, rows, width = stk.shape
    nblk = gathered.shape[0] // 2
    full = width // LANES - 1
    groups = G_ATT
    packed = full * HALF + HALF // 2
    return pl.pallas_call(
        functools.partial(attend_kernel, groups, heads),
        grid_spec=pltpu.PrefetchScalarGridSpec(
            num_scalar_prefetch=4,
            grid=(tokens // groups,),
            in_specs=[pl.BlockSpec(memory_space=pl.ANY), pl.BlockSpec(memory_space=pl.ANY)],
            out_specs=[
                pl.BlockSpec((2 * groups, heads, BLOCK), lambda i, *_: (i, 0, 0)),
                pl.BlockSpec((groups * heads, 2 * BLOCK), lambda i, *_: (i, 0)),
                pl.BlockSpec((groups, PICK * BLOCK), lambda i, *_: (i, 0)),
                pl.BlockSpec(memory_space=pl.ANY),
                pl.BlockSpec(memory_space=pl.ANY),
            ],
            scratch_shapes=[
                pltpu.VMEM((2 * nblk, HALF, width), jnp.bfloat16),
                pltpu.VMEM((2 * nblk, HALF // 2, LANES), jnp.bfloat16),
                pltpu.VMEM((tokens, rows, width), jnp.bfloat16),
                pltpu.VMEM((2 * tokens + 1, rows, BLOCK), jnp.float32),
                pltpu.VMEM((nblk, BLOCK, width), jnp.float32),
                pltpu.VMEM((2 * BLOCK, width), jnp.float32),
                pltpu.SemaphoreType.DMA((2 * full + 2,)),
            ],
        ),
        out_shape=[
            jax.ShapeDtypeStruct((2 * tokens, heads, BLOCK), jnp.float32),
            jax.ShapeDtypeStruct((tokens * heads, 2 * BLOCK), jnp.bfloat16),
            jax.ShapeDtypeStruct((tokens, PICK * BLOCK), jnp.float32),
            jax.ShapeDtypeStruct((nblk, packed, LANES), jnp.bfloat16),
            jax.ShapeDtypeStruct((nblk, packed, LANES), jnp.bfloat16),
        ],
        compiler_params=pltpu.CompilerParams(vmem_limit_bytes=VMEM_LIMIT),
        cost_estimate=pl.CostEstimate(
            flops=60_000_000_000, bytes_accessed=50_000_000, transcendentals=3_000_000
        ),
        name="attend",
    )(picks, own, tiles, pairs, stk, gathered)


def query_grad_kernel(groups, heads, own_ref, tile_ref, pair_ref, dsx_ref, dsh_ref, lat_ref, dq_ref, keys, tails, total, sem):
    own = own_ref[0]
    npairs = dsx_ref.shape[0]
    width = keys.shape[2]
    finish = load_keys(lat_ref, keys, tails, sem)

    def zero(t, carry):
        total[t] = jnp.zeros(total.shape[1:], jnp.float32)
        return carry

    lax.fori_loop(0, total.shape[0], zero, 0)
    finish()

    def tile_pair(i, carry):
        for u in range(2):
            tile = 2 * i + u
            pairs = [pair_ref[tile * PAIRS + k] for k in range(PAIRS)]
            lhs = jnp.concatenate([dsx_ref[jnp.minimum(p, npairs - 1)] for p in pairs], axis=0)
            out = dot(lhs.astype(jnp.bfloat16), block_of(keys, tile_ref[1 + tile]), 1, 0)
            for k, p in enumerate(pairs):
                total[p // 2] += out[k * heads : (k + 1) * heads]
        return carry

    lax.fori_loop(0, tile_ref[0], tile_pair, 0)
    ksh = jnp.concatenate([block_of(keys, own), block_of(keys, 0)], axis=0)

    def shared(i, carry):
        part = pl.ds(pl.multiple_of(i * groups * heads, groups * heads), groups * heads)
        out = dot(dsh_ref[part, :], ksh, 1, 0)
        out = out + total[pl.ds(i * groups, groups)].reshape(groups * heads, width)
        dq_ref[part, :] = out.astype(jnp.bfloat16)
        return carry

    lax.fori_loop(0, dsh_ref.shape[0] // (groups * heads), shared, 0)


def query_grad_call(own, tiles, pairs, dsx, dsh, gathered, heads, width):
    tokens = dsx.shape[0] // 2
    nblk = gathered.shape[0] // 2
    full = width // LANES - 1
    vmem = pl.BlockSpec(memory_space=pltpu.VMEM)
    smem = pl.BlockSpec(memory_space=pltpu.SMEM)
    return pl.pallas_call(
        functools.partial(query_grad_kernel, G_ATT, heads),
        in_specs=[smem, smem, smem, vmem, vmem, pl.BlockSpec(memory_space=pl.ANY)],
        out_specs=vmem,
        out_shape=jax.ShapeDtypeStruct((tokens * heads, width), jnp.bfloat16),
        scratch_shapes=[
            pltpu.VMEM((2 * nblk, HALF, width), jnp.bfloat16),
            pltpu.VMEM((2 * nblk, HALF // 2, LANES), jnp.bfloat16),
            pltpu.VMEM((tokens + 1, heads, width), jnp.float32),
            pltpu.SemaphoreType.DMA((full + 1,)),
        ],
        compiler_params=pltpu.CompilerParams(vmem_limit_bytes=VMEM_LIMIT),
        cost_estimate=pl.CostEstimate(
            flops=12_000_000_000, bytes_accessed=25_000_000, transcendentals=0
        ),
        name="query_grad",
    )(own, tiles, pairs, dsx, dsh, gathered)


def softplus(x):
    return jnp.maximum(x, 0.0) + jnp.log(1.0 + jnp.exp(-jnp.abs(x)))


def weight_column(wt, t):
    lane = lax.broadcasted_iota(jnp.int32, wt.shape, 1)
    return jnp.sum(jnp.where(lane == t, wt, 0.0), axis=1, keepdims=True)


def index_logits_kernel(groups, heads, picks_ref, own_ref, iq_ref, wt_ref, ik_ref, out_ref):
    step = pl.program_id(0)
    own = own_ref[0]
    ksh = jnp.concatenate([block_of(ik_ref, own), block_of(ik_ref, 0)], axis=0)
    gate_sh = dot(iq_ref[...], ksh, 1, 1)
    wt = wt_ref[...]
    outs = []
    for g in range(groups):
        t = step * groups + g
        e0 = jnp.maximum(picks_ref[t * PICK + 2], 0)
        e1 = jnp.maximum(picks_ref[t * PICK + 3], 0)
        kx = jnp.concatenate([block_of(ik_ref, e0), block_of(ik_ref, e1)], axis=0)
        gate_x = dot(iq_ref[pl.ds(g * heads, heads), :], kx, 1, 1)
        gate = jnp.concatenate([gate_sh[g * heads : (g + 1) * heads], gate_x], axis=1)
        w = weight_column(wt, t)
        outs.append(jnp.sum(w * softplus(gate), axis=0, keepdims=True))
    out_ref[...] = jnp.concatenate(outs, axis=0) * inv_root


def index_back_kernel(
    groups, heads, picks_ref, own_ref, iq_ref, wt_ref, ik_ref, logit_ref, tgt_ref, diq_ref, dwt_ref, dik_ref, acc, acc_sh
):
    step = pl.program_id(0)
    own = own_ref[0]

    @pl.when(step == 0)
    def _():
        acc[...] = jnp.zeros(acc.shape, jnp.float32)
        acc_sh[...] = jnp.zeros(acc_sh.shape, jnp.float32)
        dwt_ref[...] = jnp.zeros(dwt_ref.shape, jnp.float32)

    bias = jnp.concatenate(
        [mask_row(picks_ref, step * groups + g, step * groups + g) for g in range(groups)], axis=0
    )
    logits = logit_ref[...] + bias
    top = jnp.max(logits, axis=1, keepdims=True)
    expo = jnp.exp(logits - top)
    soft = expo * (1.0 / jnp.sum(expo, axis=1, keepdims=True))
    d_logit_all = jnp.where(bias == 0.0, kl_weight * (soft - tgt_ref[...] * (1.0 / H)), 0.0)

    ksh = jnp.concatenate([block_of(ik_ref, own), block_of(ik_ref, 0)], axis=0)
    gate_sh = dot(iq_ref[...], ksh, 1, 1)
    wt = wt_ref[...]
    lane = lax.broadcasted_iota(jnp.int32, wt.shape, 1)
    dwt = dwt_ref[...]
    dg_list, dx_list = [], []
    for g in range(groups):
        t = step * groups + g
        e0 = jnp.maximum(picks_ref[t * PICK + 2], 0)
        e1 = jnp.maximum(picks_ref[t * PICK + 3], 0)
        kx = jnp.concatenate([block_of(ik_ref, e0), block_of(ik_ref, e1)], axis=0)
        iq_g = iq_ref[pl.ds(g * heads, heads), :]
        gate_x = dot(iq_g, kx, 1, 1)
        gate = jnp.concatenate([gate_sh[g * heads : (g + 1) * heads], gate_x], axis=1)
        w = weight_column(wt, t)
        d_logit = d_logit_all[g : g + 1]
        small = jnp.exp(-jnp.abs(gate))
        denom = 1.0 + small
        soft_gate = jnp.maximum(gate, 0.0) + jnp.log(denom)
        sig = jnp.where(gate >= 0.0, 1.0, small) / denom
        dw = jnp.sum(d_logit * soft_gate, axis=1, keepdims=True) * inv_root
        dwt = jnp.where(lane == t, dw, dwt)
        d_gate = (d_logit * (w * inv_root) * sig).astype(jnp.bfloat16)
        gx = d_gate[:, 2 * BLOCK :]
        dx_list.append(dot(gx, kx, 1, 0))
        upd = dot(gx, iq_g, 0, 0)
        acc[e0] += upd[:BLOCK]
        acc[e1] += upd[BLOCK:]
        dg_list.append(d_gate[:, : 2 * BLOCK])
    dwt_ref[...] = dwt
    dg_sh = jnp.concatenate(dg_list, axis=0)
    diq = dot(dg_sh, ksh, 1, 0) + jnp.concatenate(dx_list, axis=0)
    diq_ref[...] = diq.astype(jnp.bfloat16)
    acc_sh[...] += dot(dg_sh, iq_ref[...], 0, 0)

    @pl.when(step == pl.num_programs(0) - 1)
    def _():
        acc[own] += acc_sh[pl.ds(0, BLOCK), :]
        acc[0] += acc_sh[pl.ds(BLOCK, BLOCK), :]
        dik_ref[...] = acc[...].astype(jnp.bfloat16)


def index_logits_call(picks, own, iq, wt, gathered, heads, tokens):
    groups = G_IDX
    span = PICK * BLOCK
    return pl.pallas_call(
        functools.partial(index_logits_kernel, groups, heads),
        grid_spec=pltpu.PrefetchScalarGridSpec(
            num_scalar_prefetch=2,
            grid=(tokens // groups,),
            in_specs=[
                pl.BlockSpec((groups * heads, iq.shape[1]), lambda i, *_: (i, 0)),
                pl.BlockSpec(wt.shape, lambda i, *_: (0, 0)),
                pl.BlockSpec((gathered.shape[0], HALF, LANES), lambda i, *_: (0, 0, 0)),
            ],
            out_specs=pl.BlockSpec((groups, span), lambda i, *_: (i, 0)),
        ),
        out_shape=jax.ShapeDtypeStruct((tokens, span), jnp.float32),
        compiler_params=pltpu.CompilerParams(vmem_limit_bytes=VMEM_LIMIT),
        cost_estimate=pl.CostEstimate(
            flops=10_000_000_000, bytes_accessed=4_000_000, transcendentals=6_000_000
        ),
        name="index_logits",
    )(picks, own, iq, wt, gathered)


def index_back_call(picks, own, iq, wt, gathered, logits, target, heads, tokens):
    groups = G_IDX
    span = PICK * BLOCK
    width = iq.shape[1]
    nblk = gathered.shape[0] // 2
    return pl.pallas_call(
        functools.partial(index_back_kernel, groups, heads),
        grid_spec=pltpu.PrefetchScalarGridSpec(
            num_scalar_prefetch=2,
            grid=(tokens // groups,),
            in_specs=[
                pl.BlockSpec((groups * heads, width), lambda i, *_: (i, 0)),
                pl.BlockSpec(wt.shape, lambda i, *_: (0, 0)),
                pl.BlockSpec((gathered.shape[0], HALF, LANES), lambda i, *_: (0, 0, 0)),
                pl.BlockSpec((groups, span), lambda i, *_: (i, 0)),
                pl.BlockSpec((groups, span), lambda i, *_: (i, 0)),
            ],
            out_specs=[
                pl.BlockSpec((groups * heads, width), lambda i, *_: (i, 0)),
                pl.BlockSpec((heads, tokens), lambda i, *_: (0, 0)),
                pl.BlockSpec((nblk, BLOCK, width), lambda i, *_: (0, 0, 0)),
            ],
            scratch_shapes=[
                pltpu.VMEM((nblk, BLOCK, width), jnp.float32),
                pltpu.VMEM((2 * BLOCK, width), jnp.float32),
            ],
        ),
        out_shape=[
            jax.ShapeDtypeStruct((tokens * heads, width), jnp.bfloat16),
            jax.ShapeDtypeStruct((heads, tokens), jnp.float32),
            jax.ShapeDtypeStruct((nblk, BLOCK, width), jnp.bfloat16),
        ],
        compiler_params=pltpu.CompilerParams(vmem_limit_bytes=VMEM_LIMIT),
        cost_estimate=pl.CostEstimate(
            flops=20_000_000_000, bytes_accessed=8_000_000, transcendentals=6_000_000
        ),
        name="index_back",
    )(picks, own, iq, wt, gathered, logits, target)


def tile_lists(picks):
    nblk = 64
    block = jnp.maximum(picks[:, 2:], 0).reshape(-1)
    npairs = block.shape[0]
    ntiles = -(-(npairs // PAIRS + nblk) // 2) * 2
    hot = (block[:, None] == jnp.arange(nblk)[None, :]).astype(jnp.int32)
    order = jnp.arange(npairs)
    same = (block[:, None] == block[None, :]) & (order[:, None] > order[None, :])
    rank = jnp.sum(same.astype(jnp.int32), axis=1)
    count = jnp.sum(hot, axis=0)
    padded = (count + PAIRS - 1) // PAIRS * PAIRS
    b = jnp.arange(nblk)
    start = jnp.sum(jnp.where(b[None, :] < b[:, None], padded[None, :], 0), axis=1)
    place = jnp.sum(hot * start[None, :], axis=1) + rank
    slots = jnp.arange(ntiles * PAIRS)
    found = place[None, :] == slots[:, None]
    pairs = jnp.sum(jnp.where(found, order[None, :] - npairs, 0), axis=1) + npairs
    ends = start + padded
    tile = jnp.arange(ntiles) * PAIRS
    owner = jnp.sum((ends[None, :] <= tile[:, None]).astype(jnp.int32), axis=1)
    owner = jnp.minimum(owner, nblk - 1)
    steps = (jnp.sum(padded) // PAIRS + 1) // 2
    tiles = jnp.concatenate([steps.reshape(1), owner])
    return tiles.astype(jnp.int32), pairs.astype(jnp.int32)


def axis_groups(stride):
    return [[b + k * stride for k in range(4)] for b in range(64) if (b // stride) % 4 == 0]


def swap_heads(x):
    return lax.ppermute(x, "head", [(0, 1), (1, 0)])


def head_sum(x):
    return x + swap_heads(x)


def join_halves(x, core):
    other = swap_heads(x)
    first = jnp.where(core == 0, x, other)
    second = jnp.where(core == 0, other, x)
    return jnp.concatenate([first, second], axis=0)


def pack_half(x):
    full = x.shape[1] // LANES
    tiles = x[:, : full * LANES].reshape(HALF, full, LANES).transpose(1, 0, 2).reshape(-1, LANES)
    last = x[:, full * LANES :]
    return jnp.concatenate([tiles, jnp.concatenate([last[: HALF // 2], last[HALF // 2 :]], axis=1)], axis=0)


def unpack_half(x):
    full = x.shape[0] // HALF
    tiles = x[: full * HALF].reshape(full, HALF, LANES).transpose(1, 0, 2).reshape(HALF, -1)
    last = x[full * HALF :]
    last = jnp.concatenate([last[:, :HALF], last[:, HALF:]], axis=0)
    return jnp.concatenate([tiles, last], axis=1)


def per_device(queries, latent, d_out, index_q, index_w, index_k, picks):
    rows, heads, width = queries.shape
    vwidth = d_out.shape[2]
    iheads, iwidth = index_q.shape[1:]
    wide = -(-width // LANES) * LANES
    core = lax.axis_index("head").astype(jnp.int32)
    own = jnp.stack([lax.axis_index("seq").astype(jnp.int32), core])
    picks_flat = picks.reshape(-1)

    lat_half = lax.dynamic_slice_in_dim(latent, core * HALF, HALF, 0)
    ik_half = lax.dynamic_slice_in_dim(index_k, core * HALF, HALF, 0)
    mine = jnp.concatenate([ik_half, pack_half(lat_half)], axis=0)
    gathered = lax.all_gather(mine, ("seq", "head"), axis=0, tiled=False)

    tiles, pairs = tile_lists(picks)
    stk = jnp.concatenate(
        [
            jnp.pad(queries, ((0, 0), (0, 0), (0, wide - width))),
            jnp.pad(d_out, ((0, 0), (0, 0), (0, wide - vwidth))),
        ],
        axis=1,
    )
    dsx, dsh, target_part, keep, send = attend_call(picks_flat, own, tiles, pairs, stk, gathered, heads)
    lat_sum = keep + swap_heads(send)
    for stride in (16, 4, 1):
        lat_sum = lax.psum_scatter(
            lat_sum, "seq", scatter_dimension=0, tiled=True, axis_index_groups=axis_groups(stride)
        )
    iq = index_q.reshape(rows * iheads, iwidth)
    wt = index_w.astype(jnp.float32).T
    logits = head_sum(index_logits_call(picks_flat, own, iq, wt, gathered, iheads, rows))
    target = head_sum(target_part)
    diq, dwt, dik = index_back_call(
        picks_flat, own, iq, wt, gathered, logits, target, iheads, rows
    )
    dik = dik.reshape(-1, 2, HALF, iwidth)
    ik_keep = lax.dynamic_index_in_dim(dik, core, 1, keepdims=False)
    ik_send = lax.dynamic_index_in_dim(dik, 1 - core, 1, keepdims=False)
    ik_sum = ik_keep + swap_heads(ik_send)
    ik_sum = lax.all_to_all(ik_sum, "seq", 0, 0, tiled=True)
    ik_sum = jnp.sum(ik_sum.astype(jnp.float32), axis=0).astype(jnp.bfloat16)
    dq = query_grad_call(own, tiles, pairs, dsx, dsh, gathered, heads, wide)

    d_latent = join_halves(unpack_half(lat_sum[0]), core)
    d_index_k = join_halves(ik_sum, core)
    d_queries = dq.reshape(rows, heads, wide)[:, :, :width]
    return (d_queries, d_latent, diq.reshape(rows, iheads, iwidth), dwt.T, d_index_k)


def solution(mesh):
    return jax.shard_map(
        per_device,
        mesh=mesh,
        in_specs=(
            P("seq", "head", None),
            P("seq", None),
            P("seq", "head", None),
            P("seq", "head", None),
            P("seq", "head"),
            P("seq", None),
            P("seq", None),
        ),
        out_specs=(
            P("seq", "head", None),
            P("seq", None),
            P("seq", "head", None),
            P("seq", "head"),
            P("seq", None),
        ),
        check_vma=False,
    )
```

time: 1710 us -> 323 us (0.19)
  local copies, waits for them, and re-layouts: 521 us -> 28.7 us
  waiting for transfers between devices: 561 us -> 79.8 us
  other arithmetic: 354 us -> 28.8 us
  matrix products: 181 us -> 0 us
  Pallas kernels: 0 us -> 153 us
  blocking collectives: 53.3 us -> 0 us
    reduce_scatter x2 -> x3, waiting for transfers between devices: 389 us -> 0.03 us  [per_device(): lax.psum_scatter(lat_sum, 'seq', scatter_dimension=0, tiled=True, axis_in...]
    reshape x14 -> x2, local copies, waits for them, and re-layouts: 247 us -> 0.78 us  [the longest x1 0.64 us: per_device(): picks_flat = picks.reshape(-1)]
    scatter-add x24 -> x0, other arithmetic: 238 us -> none  [the longest x4 149 us: attend(): acc_lat.at[extra_blk].add(upd_extra.reshape(group, PICK - 2, BLOCK, width))]
    dot_general x56 -> x0, matrix products: 181 us -> none  [the longest x4 41.8 us: attend(): jnp.einsum('ths,tsd->thd', dscore[:, :, shared_span:], lat_extra, preferr...]
    pallas_call x0 -> x4, Pallas kernels: none -> 153 us  [the longest x1 74.7 us: attend_call(): pl.pallas_call(functools.partial(attend_kernel, groups, heads), grid_spec...]
    gather x16 -> x0, local copies, waits for them, and re-layouts: 115 us -> none  [the longest x8 95 us: attend(): lat_extra = lat_blocks[extra_blk].reshape(group, -1, width)]
    all_gather x2 -> x1, waiting for transfers between devices: 141 us -> 46.7 us  [per_device(): gathered = lax.all_gather(mine, ('seq', 'head'), axis=0, tiled=False)]
    dot_general x4 -> x0, local copies, waits for them, and re-layouts: 93.7 us -> none  [attend(): jnp.einsum('ths,thd->tsd', grads[:, :, shared_span:], stacked, preferred_...]
  transfers between devices with their start and end apart: 6 -> 11, of which waited for: 6 -> 6; matrix products, arithmetic and copies ran while one was open for 12% -> 14% of each run, Pallas kernels for 0% -> 24%
where the time goes in v1:
time: 323 us; the launch traced here: 321 us
  Pallas kernels  153 us (47%)
  waiting for transfers between devices  79.8 us (25%)
  other arithmetic  28.8 us (9%)
  local copies, waits for them, and re-layouts  28.7 us (9%)
  between operations  16.6 us (5%)
  starting transfers between devices  14.4 us (4%)
    pallas_call x1, Pallas kernels, attend_call(): pl.pallas_call(functools.partial(attend_kernel, groups, heads), grid_spec...  74.7 us
    all_gather x1, waiting for transfers between devices, per_device(): gathered = lax.all_gather(mine, ('seq', 'head'), axis=0, tiled=False)  46.7 us
    pallas_call x1, Pallas kernels, index_back_call(): pl.pallas_call(functools.partial(index_back_kernel, groups, heads), grid_...  39.3 us
    pallas_call x1, Pallas kernels, query_grad_call(): pl.pallas_call(functools.partial(query_grad_kernel, G_ATT, heads), in_spe...  25.9 us
    unnamed x13, local copies, waits for them, and re-layouts  22.5 us
    all_to_all x1, waiting for transfers between devices, per_device(): ik_sum = lax.all_to_all(ik_sum, 'seq', 0, 0, tiled=True)  21.2 us
    pallas_call x1, Pallas kernels, index_logits_call(): pl.pallas_call(functools.partial(index_logits_kernel, groups, heads), gri...  12.9 us
    ppermute x6, waiting for transfers between devices, swap_heads(): return lax.ppermute(x, 'head', [(0, 1), (1, 0)])  11.8 us
  transfers between devices with their start and end apart: 11, of which 6 were waited for; matrix products, arithmetic and copies ran while one was open for 14% of the time, Pallas kernels for 24%

profile of v1, /device:TPU:1, one launch (start us, length us, event | category | flops | bytes accessed | tf_op | source)
XLA Modules:
  0.0 321.1 jit_solution(1512204763976260252)
XLA Ops:
  7.2 1.0 constant_dynamic-slice_fusion.1
  8.2 0.9 fusion.7
  9.5 0.7 maximum_maximum_fusion
  14.6 0.8 copy.35
  16.2 11.0 %copy.36 = bf16[128,40,576]{2,1,0:T(8,128)(2,1)} copy(bf16[128,40,576]{0,2,1:T(8,128)(2,1)} %param.7) | data formatting | bytes 11796480 | tf_op args[0]
  29.5 11.4 %fusion.2.stk_hbm = bf16[128,80,640]{2,1,0:T(8,128)(2,1)} fusion(bf16[128,40,512]{2,1,0:T(8,128)(2,1)} %param.9, bf16[128,40,576]{2,1,0:T(8,128)(2,1)} %copy.36), kind=kLoop, calls=%fused_computation.4 | loop fusion | flops 52428800 | bytes 24248320 | tf_op jit(solution)/shard_map/concatenate | solution.py:523
  40.9 46.7 %all-gather.3.cloned.1.call-done = bf16[45056,128]{1,0:T(8,128)(2,1)} async-done(((bf16[352,128]{1,0:T(8,128)(2,1)}), bf16[45056,128]{1,0:T(8,128)(2,1)}) %all-gather.3.cloned.1.call-update) | async-done | bytes 11534352 | tf_op jit(solution)/shard_map/all_gather | solution.py:520
  87.6 74.7 %attend.1 = (f32[256,40,128]{2,1,0:T(8,128)}, bf16[5120,256]{1,0:T(8,128)(2,1)}, f32[128,512]{1,0:T(8,128)}, bf16[64,288,128]{2,1,0:T(8,128)(2,1)}, bf16[64,288,128]{2,1,0:T(8,128)(2,1)}) custom-call(s32[512]{0:T(512)} %reshape.85.picks_ref, s32[2]{0:T(128)} %pad_add_fusion.1.own_ref, s32[129]{0:T(256)} %pad_add_fusion.tile_ref, ...), custom_call_target="tpu_custom_call" | custom-call | flops 60000002048 | bytes 50000000 | tf_op jit(solution)/shard_map/attend/pallas_call | solution.py:194
  162.6 7.9 %collective-permute-done = bf16[64,288,128]{2,1,0:T(8,128)(2,1)S(1)} collective-permute-done((bf16[64,288,128]{2,1,0:T(8,128)(2,1)}, bf16[64,288,128]{2,1,0:T(8,128)(2,1)S(1)}, u32[]{:S(2)}, u32[]{:S(2)}) %collective-permute-start) | collective-permute-done | bytes 4718624 | tf_op jit(solution)/shard_map/ppermute | solution.py:479
  170.5 5.7 %add.94 = bf16[64,288,128]{2,1,0:T(8,128)(2,1)} add(bf16[64,288,128]{2,1,0:T(8,128)(2,1)} %get-tuple-element.15, bf16[64,288,128]{2,1,0:T(8,128)(2,1)S(1)} %collective-permute-done) | non-fusion elementwise | flops 2359296 | bytes 14155776 | tf_op jit(solution)/shard_map/add | solution.py:531
  177.2 12.9 %index_logits.1 = f32[128,512]{1,0:T(8,128)} custom-call(s32[512]{0:T(512)} %reshape.85.picks_ref, s32[2]{0:T(128)} %pad_add_fusion.1.own_ref, bf16[4096,128]{1,0:T(8,128)(2,1)} %bitcast.38, f32[32,128]{1,0:T(8,128)} %convert_bitcast_fusion.wt_ref, bf16[128,352,128]{2,1,0:T(8,128)(2,1)} %bitcast.35), custom_call_target="tpu_custom_call" | custom-call | flops 10000000000 | bytes 4000000 | tf_op jit(solution)/shard_map/index_logits/pallas_call | solution.py:387
  190.4 0.8 add.96.tgt_ref
  191.9 1.7 add.95.logit_ref
  193.6 39.3 %index_back.1 = (bf16[4096,128]{1,0:T(8,128)(2,1)}, f32[32,128]{1,0:T(8,128)}, bf16[64,128,128]{2,1,0:T(8,128)(2,1)}) custom-call(s32[512]{0:T(512)} %reshape.85.picks_ref, s32[2]{0:T(128)} %pad_add_fusion.1.own_ref, bf16[4096,128]{1,0:T(8,128)(2,1)} %bitcast.39, f32[32,128]{1,0:T(8,128)} %convert_bitcast_fusion.wt_ref, bf16[128,352,128]{2,1,0:T(8,128)(2,1)} %bitcast.36, ...), custom_call_target="tpu_custom_call" | custom-call | flops 20000000000 | bytes 8000000 | tf_op jit(solution)/shard_map/index_back/pallas_call | solution.py:413
  232.9 1.3 dynamic-slice_bitcast_fusion
  234.5 2.5 collective-permute-done.4
  237.0 2.3 bitcast_add_fusion
  239.3 11.6 %all-to-all-start = ((bf16[64,64,128]{2,1,0:T(8,128)(2,1)}), bf16[64,64,128]{2,1,0:T(8,128)(2,1)S(1)}, u32[]{:S(2)}, u32[]{:S(2)}) async-start(bf16[64,64,128]{2,1,0:T(8,128)(2,1)} %bitcast_add_fusion), calls=%async_computation.3 | async-start | bytes 2097152 | tf_op jit(solution)/shard_map/all_to_all | solution.py:547
  250.9 21.2 %all-to-all-done = bf16[64,64,128]{2,1,0:T(8,128)(2,1)S(1)} async-done(((bf16[64,64,128]{2,1,0:T(8,128)(2,1)}), bf16[64,64,128]{2,1,0:T(8,128)(2,1)S(1)}, u32[]{:S(2)}, u32[]{:S(2)}) %all-to-all-start) | async-done | bytes 1048608 | tf_op jit(solution)/shard_map/all_to_all | solution.py:547
  272.3 1.4 collective-permute-start.5
  273.8 25.9 %query_grad.1 = bf16[5120,640]{1,0:T(8,128)(2,1)} custom-call(s32[2]{0:T(128)} %pad_add_fusion.1.own_ref, s32[129]{0:T(256)} %pad_add_fusion.tile_ref, s32[512]{0:T(512)} %broadcast_add_fusion.pair_ref, f32[256,40,128]{2,1,0:T(8,128)} %get-tuple-element.13.dsx_ref, bf16[5120,256]{1,0:T(8,128)(2,1)} %get-tuple-element.14.dsh_ref, bf16[128,352,128]{2,1,0:T(8,128)(2,1)} %bitcast.37), custom_call_target="tpu_custom_call" | custom-call | flops 12000000000 | bytes 25000000 | tf_op jit(solution)/shard_map/query_grad/pallas_call | solution.py:274
  299.7 10.6 %copy.46 = bf16[128,40,576]{0,2,1:T(8,128)(2,1)} copy(bf16[128,40,576]{2,1,0:T(8,128)(2,1)} %bitcast.25) | data formatting | bytes 11796480
  310.4 0.8 slice.45
  313.8 0.8 pad_maximum_fusion.1
  (63 shorter events, 10.6 us)
Async XLA Ops:
  7.2 2.3 copy-start
  7.2 80.4 %all-gather.3.cloned.1.call-start = ((), (), s32[]{:S(2)}) async-start(), calls=%async_computation.7 | async-start | bytes 11624448 | tf_op jit(solution)/shard_map/all_gather | solution.py:520
  10.2 222.6 %reduce-scatter.4.cloned.1.call-start = ((), (), s32[]{:S(2)}) async-start(), calls=%async_computation.4 | async-start | bytes 5898240 | tf_op jit(solution)/shard_map/reduce_scatter | solution.py:533
  162.3 8.2 %collective-permute-start = (bf16[64,288,128]{2,1,0:T(8,128)(2,1)}, bf16[64,288,128]{2,1,0:T(8,128)(2,1)S(1)}, u32[]{:S(2)}, u32[]{:S(2)}) collective-permute-start(bf16[64,288,128]{2,1,0:T(8,128)(2,1)} %get-tuple-element.16), channel_id=1, source_target_pairs={{0,1},{1,0},{2,3},{3,2},{4,5},{5,4},{6,7},{7,6},{8,9},{9,8},{10,11... | collective-permute-start | bytes 14155784 | tf_op jit(solution)/shard_map/ppermute | solution.py:479
  170.5 5.8 %copy-start.3 = (bf16[128,32]{0,1:T(8,128)(2,1)S(1)}, bf16[128,32]{0,1:T(8,128)(2,1)}, u32[]{:S(2)}) copy-start(bf16[128,32]{0,1:T(8,128)(2,1)} %param.11) | copy-start | bytes 24580
  170.5 6.4 %copy-start.2 = (f32[128,512]{1,0:T(8,128)S(1)}, f32[128,512]{1,0:T(8,128)}, u32[]{:S(2)}) copy-start(f32[128,512]{1,0:T(8,128)} %get-tuple-element.17) | copy-start | bytes 786436
  176.3 97.5 %reduce-scatter.6.cloned.1.call-start = ((), (), s32[]{:S(2)}) async-start(), calls=%async_computation.5 | async-start | bytes 1474560 | tf_op jit(solution)/shard_map/reduce_scatter | solution.py:533
  176.9 13.4 %collective-permute-start.3 = (f32[128,512]{1,0:T(8,128)S(1)}, f32[128,512]{1,0:T(8,128)S(1)}, u32[]{:S(2)}, u32[]{:S(2)}) collective-permute-start(f32[128,512]{1,0:T(8,128)S(1)} %copy-done.2), channel_id=1, source_target_pairs={{0,1},{1,0},{2,3},{3,2},{4,5},{5,4},{6,7},{7,6},{8,9},{9,8},{10,11... | collective-permute-start | bytes 786440 | tf_op jit(solution)/shard_map/ppermute | solution.py:479
  190.1 1.7 collective-permute-start.2
  234.2 2.7 collective-permute-start.4
  239.3 32.8 %all-to-all-start = ((bf16[64,64,128]{2,1,0:T(8,128)(2,1)}), bf16[64,64,128]{2,1,0:T(8,128)(2,1)S(1)}, u32[]{:S(2)}, u32[]{:S(2)}) async-start(bf16[64,64,128]{2,1,0:T(8,128)(2,1)} %bitcast_add_fusion), calls=%async_computation.3 | async-start | bytes 2097152 | tf_op jit(solution)/shard_map/all_to_all | solution.py:547
  250.9 59.5 %reduce-scatter.8.cloned.1.call-start = ((), (), s32[]{:S(2)}) async-start(), calls=%async_computation.6 | async-start | bytes 368640 | tf_op jit(solution)/shard_map/reduce_scatter | solution.py:533
  272.3 38.0 %collective-permute-start.5 = (bf16[64,128]{1,0:T(8,128)(2,1)S(1)}, bf16[64,128]{1,0:T(8,128)(2,1)S(1)}, u32[]{:S(2)}, u32[]{:S(2)}) collective-permute-start(bf16[64,128]{1,0:T(8,128)(2,1)S(1)} %reduce_sum.82), channel_id=1, source_target_pairs={{0,1},{1,0},{2,3},{3,2},{4,5},{5,4},{6,7},{7,6},{8,9},{9,8},{10,11... | collective-permute-start | bytes 49160 | tf_op jit(solution)/shard_map/ppermute | solution.py:479
  299.7 14.9 %copy-start.1 = (bf16[128,128]{1,0:T(8,128)(2,1)S(1)}, bf16[128,128]{1,0:T(8,128)(2,1)}, u32[]{:S(2)}) copy-start(bf16[128,128]{1,0:T(8,128)(2,1)} %param.12) | copy-start | bytes 98308
  312.3 1.5 collective-permute-start.1
Sparse Core Ops, SparseCore 0:
  11.6 75.9 all-gather.2
  176.4 53.6 reduce-scatter.3
  233.0 29.6 reduce-scatter.5
  273.9 15.7 reduce-scatter.7

commit v2 on v1

--- a/solution.py
+++ b/solution.py
@@ -20,6 +20,7 @@
 
 G_ATT = 8
 G_IDX = 8
+UNROLL = 4
 PAIRS = 4
 HALF = BLOCK // 2
 VMEM_LIMIT = 58 * 1024 * 1024
@@ -45,7 +46,7 @@
     full = keys.shape[2] // LANES - 1
     copies = [
         pltpu.make_async_copy(
-            lat_ref.at[:, pl.ds((c + 1) * HALF, HALF), :],
+            lat_ref.at[:, pl.ds(c * HALF, HALF), :],
             keys.at[:, :, pl.ds(c * LANES, LANES)],
             sem.at[c],
         )
@@ -53,7 +54,7 @@
     ]
     copies.append(
         pltpu.make_async_copy(
-            lat_ref.at[:, pl.ds((full + 1) * HALF, HALF // 2), :], tails, sem.at[full]
+            lat_ref.at[:, pl.ds(full * HALF, HALF // 2), :], tails, sem.at[full]
         )
     )
     for cp in copies:
@@ -69,7 +70,7 @@
             keys[i, :, pl.ds(full * LANES, LANES)] = jnp.concatenate([low, high], axis=0)
             return carry
 
-        lax.fori_loop(0, keys.shape[0], unpack, 0, unroll=4)
+        lax.fori_loop(0, keys.shape[0], unpack, 0, unroll=8)
 
     return finish
 
@@ -89,9 +90,16 @@
 
     @pl.when(step == 0)
     def _():
-        load_stk = pltpu.make_async_copy(stk_hbm, stk, sem.at[full + 1])
+        chunk = tokens // full
+        load_stk = [
+            pltpu.make_async_copy(
+                stk_hbm.at[pl.ds(c * chunk, chunk)], stk.at[pl.ds(c * chunk, chunk)], sem.at[full + 1 + c]
+            )
+            for c in range(full)
+        ]
         finish = load_keys(lat_ref, keys, tails, sem)
-        load_stk.start()
+        for cp in load_stk:
+            cp.start()
 
         def zero(b, carry):
             acc[b] = jnp.zeros(acc.shape[1:], jnp.float32)
@@ -100,11 +108,12 @@
         lax.fori_loop(0, nblk, zero, 0)
         acc_sh[...] = jnp.zeros(acc_sh.shape, jnp.float32)
         finish()
-        load_stk.wait()
+        for cp in load_stk:
+            cp.wait()
 
         def tile_pair(i, carry):
-            for u in range(2):
-                tile = 2 * i + u
+            for u in range(UNROLL):
+                tile = UNROLL * i + u
                 pairs = [pair_ref[tile * PAIRS + k] for k in range(PAIRS)]
                 lhs = jnp.concatenate([stk[jnp.minimum(p // 2, tokens - 1)] for p in pairs], axis=0)
                 out = dot(lhs, block_of(keys, tile_ref[1 + tile]), 1, 1)
@@ -151,36 +160,38 @@
         acc[own] += acc_sh[pl.ds(0, BLOCK), :]
         acc[0] += acc_sh[pl.ds(BLOCK, BLOCK), :]
 
-        def cast(b, carry):
-            for k, which in enumerate((core, 1 - core)):
-                part = acc[b, pl.ds(pl.multiple_of(which * HALF, HALF), HALF), :]
-                keys[k * nblk + b] = part.astype(jnp.bfloat16)
-                last = part[:, full * LANES :]
+        stores = []
+        for k, ref, which in ((0, send_ref, 1 - core), (1, keep_ref, core)):
+            rows_of = pl.ds(pl.multiple_of(which * HALF, HALF), HALF)
+            part = pl.ds(k * nblk, nblk)
+
+            def cast(b, carry):
+                half = acc[b, rows_of, :]
+                keys[k * nblk + b] = half.astype(jnp.bfloat16)
+                last = half[:, full * LANES :]
                 packed = last[: HALF // 2] + pltpu.roll(last[HALF // 2 :], HALF, 1)
                 tails[k * nblk + b] = packed.astype(jnp.bfloat16)
-            return carry
-
-        lax.fori_loop(0, nblk, cast, 0)
-        stores = []
-        for k, ref in enumerate((keep_ref, send_ref)):
-            part = pl.ds(k * nblk, nblk)
-            for c in range(full):
-                stores.append(
-                    pltpu.make_async_copy(
-                        keys.at[part, :, pl.ds(c * LANES, LANES)],
-                        ref.at[:, pl.ds(c * HALF, HALF), :],
-                        sem.at[k * (full + 1) + c],
-                    )
+                return carry
+
+            lax.fori_loop(0, nblk, cast, 0, unroll=4)
+            sent = [
+                pltpu.make_async_copy(
+                    keys.at[part, :, pl.ds(c * LANES, LANES)],
+                    ref.at[:, pl.ds(c * HALF, HALF), :],
+                    sem.at[k * (full + 1) + c],
                 )
-            stores.append(
+                for c in range(full)
+            ]
+            sent.append(
                 pltpu.make_async_copy(
                     tails.at[part],
                     ref.at[:, pl.ds(full * HALF, HALF // 2), :],
                     sem.at[k * (full + 1) + full],
                 )
             )
-        for cp in stores:
-            cp.start()
+            for cp in sent:
+                cp.start()
+            stores += sent
         for cp in stores:
             cp.wait()
 
@@ -196,7 +207,7 @@
         grid_spec=pltpu.PrefetchScalarGridSpec(
             num_scalar_prefetch=4,
             grid=(tokens // groups,),
-            in_specs=[pl.BlockSpec(memory_space=pl.ANY), pl.BlockSpec(memory_space=pl.ANY)],
+            in_specs=[pl.BlockSpec(memory_space=pl.ANY)] * 2,
             out_specs=[
                 pl.BlockSpec((2 * groups, heads, BLOCK), lambda i, *_: (i, 0, 0)),
                 pl.BlockSpec((groups * heads, 2 * BLOCK), lambda i, *_: (i, 0)),
@@ -243,8 +254,8 @@
     finish()
 
     def tile_pair(i, carry):
-        for u in range(2):
-            tile = 2 * i + u
+        for u in range(UNROLL):
+            tile = UNROLL * i + u
             pairs = [pair_ref[tile * PAIRS + k] for k in range(PAIRS)]
             lhs = jnp.concatenate([dsx_ref[jnp.minimum(p, npairs - 1)] for p in pairs], axis=0)
             out = dot(lhs.astype(jnp.bfloat16), block_of(keys, tile_ref[1 + tile]), 1, 0)
@@ -272,7 +283,7 @@
     vmem = pl.BlockSpec(memory_space=pltpu.VMEM)
     smem = pl.BlockSpec(memory_space=pltpu.SMEM)
     return pl.pallas_call(
-        functools.partial(query_grad_kernel, G_ATT, heads),
+        functools.partial(query_grad_kernel, 8, heads),
         in_specs=[smem, smem, smem, vmem, vmem, pl.BlockSpec(memory_space=pl.ANY)],
         out_specs=vmem,
         out_shape=jax.ShapeDtypeStruct((tokens * heads, width), jnp.bfloat16),
@@ -299,7 +310,7 @@
     return jnp.sum(jnp.where(lane == t, wt, 0.0), axis=1, keepdims=True)
 
 
-def index_logits_kernel(groups, heads, picks_ref, own_ref, iq_ref, wt_ref, ik_ref, out_ref):
+def index_logits_kernel(groups, heads, picks_ref, own_ref, iq_ref, wt_ref, ik_ref, gate_ref, out_ref):
     step = pl.program_id(0)
     own = own_ref[0]
     ksh = jnp.concatenate([block_of(ik_ref, own), block_of(ik_ref, 0)], axis=0)
@@ -313,13 +324,14 @@
         kx = jnp.concatenate([block_of(ik_ref, e0), block_of(ik_ref, e1)], axis=0)
         gate_x = dot(iq_ref[pl.ds(g * heads, heads), :], kx, 1, 1)
         gate = jnp.concatenate([gate_sh[g * heads : (g + 1) * heads], gate_x], axis=1)
+        gate_ref[pl.ds(g * heads, heads), :] = gate
         w = weight_column(wt, t)
         outs.append(jnp.sum(w * softplus(gate), axis=0, keepdims=True))
     out_ref[...] = jnp.concatenate(outs, axis=0) * inv_root
 
 
 def index_back_kernel(
-    groups, heads, picks_ref, own_ref, iq_ref, wt_ref, ik_ref, logit_ref, tgt_ref, diq_ref, dwt_ref, dik_ref, acc, acc_sh
+    groups, heads, picks_ref, own_ref, iq_ref, wt_ref, ik_ref, gate_ref, logit_ref, tgt_ref, diq_ref, dwt_ref, dik_ref, acc, acc_sh
 ):
     step = pl.program_id(0)
     own = own_ref[0]
@@ -340,7 +352,6 @@
     d_logit_all = jnp.where(bias == 0.0, kl_weight * (soft - tgt_ref[...] * (1.0 / H)), 0.0)
 
     ksh = jnp.concatenate([block_of(ik_ref, own), block_of(ik_ref, 0)], axis=0)
-    gate_sh = dot(iq_ref[...], ksh, 1, 1)
     wt = wt_ref[...]
     lane = lax.broadcasted_iota(jnp.int32, wt.shape, 1)
     dwt = dwt_ref[...]
@@ -351,8 +362,7 @@
         e1 = jnp.maximum(picks_ref[t * PICK + 3], 0)
         kx = jnp.concatenate([block_of(ik_ref, e0), block_of(ik_ref, e1)], axis=0)
         iq_g = iq_ref[pl.ds(g * heads, heads), :]
-        gate_x = dot(iq_g, kx, 1, 1)
-        gate = jnp.concatenate([gate_sh[g * heads : (g + 1) * heads], gate_x], axis=1)
+        gate = gate_ref[pl.ds(g * heads, heads), :]
         w = weight_column(wt, t)
         d_logit = d_logit_all[g : g + 1]
         small = jnp.exp(-jnp.abs(gate))
@@ -394,9 +404,15 @@
                 pl.BlockSpec(wt.shape, lambda i, *_: (0, 0)),
                 pl.BlockSpec((gathered.shape[0], HALF, LANES), lambda i, *_: (0, 0, 0)),
             ],
-            out_specs=pl.BlockSpec((groups, span), lambda i, *_: (i, 0)),
-        ),
-        out_shape=jax.ShapeDtypeStruct((tokens, span), jnp.float32),
+            out_specs=[
+                pl.BlockSpec((groups * heads, span), lambda i, *_: (i, 0)),
+                pl.BlockSpec((groups, span), lambda i, *_: (i, 0)),
+            ],
+        ),
+        out_shape=[
+            jax.ShapeDtypeStruct((tokens * heads, span), jnp.float32),
+            jax.ShapeDtypeStruct((tokens, span), jnp.float32),
+        ],
         compiler_params=pltpu.CompilerParams(vmem_limit_bytes=VMEM_LIMIT),
         cost_estimate=pl.CostEstimate(
             flops=10_000_000_000, bytes_accessed=4_000_000, transcendentals=6_000_000
@@ -405,7 +421,7 @@
     )(picks, own, iq, wt, gathered)
 
 
-def index_back_call(picks, own, iq, wt, gathered, logits, target, heads, tokens):
+def index_back_call(picks, own, iq, wt, gathered, gate, logits, target, heads, tokens):
     groups = G_IDX
     span = PICK * BLOCK
     width = iq.shape[1]
@@ -419,6 +435,7 @@
                 pl.BlockSpec((groups * heads, width), lambda i, *_: (i, 0)),
                 pl.BlockSpec(wt.shape, lambda i, *_: (0, 0)),
                 pl.BlockSpec((gathered.shape[0], HALF, LANES), lambda i, *_: (0, 0, 0)),
+                pl.BlockSpec((groups * heads, span), lambda i, *_: (i, 0)),
                 pl.BlockSpec((groups, span), lambda i, *_: (i, 0)),
                 pl.BlockSpec((groups, span), lambda i, *_: (i, 0)),
             ],
@@ -442,14 +459,14 @@
             flops=20_000_000_000, bytes_accessed=8_000_000, transcendentals=6_000_000
         ),
         name="index_back",
-    )(picks, own, iq, wt, gathered, logits, target)
+    )(picks, own, iq, wt, gathered, gate, logits, target)
 
 
 def tile_lists(picks):
     nblk = 64
     block = jnp.maximum(picks[:, 2:], 0).reshape(-1)
     npairs = block.shape[0]
-    ntiles = -(-(npairs // PAIRS + nblk) // 2) * 2
+    ntiles = -(-(npairs // PAIRS + nblk) // UNROLL) * UNROLL
     hot = (block[:, None] == jnp.arange(nblk)[None, :]).astype(jnp.int32)
     order = jnp.arange(npairs)
     same = (block[:, None] == block[None, :]) & (order[:, None] > order[None, :])
@@ -466,21 +483,29 @@
     tile = jnp.arange(ntiles) * PAIRS
     owner = jnp.sum((ends[None, :] <= tile[:, None]).astype(jnp.int32), axis=1)
     owner = jnp.minimum(owner, nblk - 1)
-    steps = (jnp.sum(padded) // PAIRS + 1) // 2
+    steps = (jnp.sum(padded) // PAIRS + UNROLL - 1) // UNROLL
     tiles = jnp.concatenate([steps.reshape(1), owner])
     return tiles.astype(jnp.int32), pairs.astype(jnp.int32)
 
 
-def axis_groups(stride):
-    return [[b + k * stride for k in range(4)] for b in range(64) if (b // stride) % 4 == 0]
-
-
 def swap_heads(x):
     return lax.ppermute(x, "head", [(0, 1), (1, 0)])
 
 
 def head_sum(x):
     return x + swap_heads(x)
+
+
+def add_parts(parts):
+    return jnp.sum(parts.astype(jnp.float32), axis=0).astype(parts.dtype)
+
+
+def gather_by_exchange(x, core):
+    mine = lax.all_to_all(jnp.broadcast_to(x[None], (64,) + x.shape), "seq", 0, 0, tiled=True)
+    other = swap_heads(mine)
+    first = jnp.where(core == 0, mine, other)
+    second = jnp.where(core == 0, other, mine)
+    return jnp.stack([first, second], axis=1).reshape((-1,) + x.shape)
 
 
 def join_halves(x, core):
@@ -516,8 +541,12 @@
 
     lat_half = lax.dynamic_slice_in_dim(latent, core * HALF, HALF, 0)
     ik_half = lax.dynamic_slice_in_dim(index_k, core * HALF, HALF, 0)
-    mine = jnp.concatenate([ik_half, pack_half(lat_half)], axis=0)
-    gathered = lax.all_gather(mine, ("seq", "head"), axis=0, tiled=False)
+    gathered = lax.all_gather(pack_half(lat_half), ("seq", "head"), axis=0, tiled=False)
+    ik_all = gather_by_exchange(ik_half, core)
+
+    iq = index_q.reshape(rows * iheads, iwidth)
+    wt = index_w.astype(jnp.float32).T
+    gate, logit_part = index_logits_call(picks_flat, own, iq, wt, ik_all, iheads, rows)
 
     tiles, pairs = tile_lists(picks)
     stk = jnp.concatenate(
@@ -527,30 +556,31 @@
         ],
         axis=1,
     )
-    dsx, dsh, target_part, keep, send = attend_call(picks_flat, own, tiles, pairs, stk, gathered, heads)
-    lat_sum = keep + swap_heads(send)
-    for stride in (16, 4, 1):
-        lat_sum = lax.psum_scatter(
-            lat_sum, "seq", scatter_dimension=0, tiled=True, axis_index_groups=axis_groups(stride)
-        )
-    iq = index_q.reshape(rows * iheads, iwidth)
-    wt = index_w.astype(jnp.float32).T
-    logits = head_sum(index_logits_call(picks_flat, own, iq, wt, gathered, iheads, rows))
+    own_next, logit_part = lax.optimization_barrier((own, logit_part))
+    dsx, dsh, target_part, keep, send = attend_call(picks_flat, own_next, tiles, pairs, stk, gathered, heads)
+    lat_part = keep + swap_heads(send)
+    target_part, lat_part = lax.optimization_barrier((target_part, lat_part))
+    lat_parts = lax.all_to_all(lat_part, "seq", 0, 0, tiled=True)
     target = head_sum(target_part)
+    logits = head_sum(logit_part)
     diq, dwt, dik = index_back_call(
-        picks_flat, own, iq, wt, gathered, logits, target, iheads, rows
+        picks_flat, own, iq, wt, ik_all, gate, logits, target, iheads, rows
     )
     dik = dik.reshape(-1, 2, HALF, iwidth)
     ik_keep = lax.dynamic_index_in_dim(dik, core, 1, keepdims=False)
     ik_send = lax.dynamic_index_in_dim(dik, 1 - core, 1, keepdims=False)
-    ik_sum = ik_keep + swap_heads(ik_send)
-    ik_sum = lax.all_to_all(ik_sum, "seq", 0, 0, tiled=True)
-    ik_sum = jnp.sum(ik_sum.astype(jnp.float32), axis=0).astype(jnp.bfloat16)
-    dq = query_grad_call(own, tiles, pairs, dsx, dsh, gathered, heads, wide)
-
-    d_latent = join_halves(unpack_half(lat_sum[0]), core)
+    ik_part = ik_keep + swap_heads(ik_send)
+    own_late, ik_part = lax.optimization_barrier((own, ik_part))
+    dq = query_grad_call(own_late, tiles, pairs, dsx, dsh, gathered, heads, wide)
+    dq = dq.reshape(rows, heads, wide)[:, :, :width].transpose(1, 2, 0)
+    dq, ik_part, lat_parts = lax.optimization_barrier((dq, ik_part, lat_parts))
+    ik_parts = lax.all_to_all(ik_part, "seq", 0, 0, tiled=True)
+    lat_sum = add_parts(lat_parts)
+    ik_sum = add_parts(ik_parts)
+
+    d_latent = join_halves(unpack_half(lat_sum), core)
     d_index_k = join_halves(ik_sum, core)
-    d_queries = dq.reshape(rows, heads, wide)[:, :, :width]
+    d_queries = dq.transpose(2, 0, 1)
     return (d_queries, d_latent, diq.reshape(rows, iheads, iwidth), dwt.T, d_index_k)
 
 

time: 323 us -> 288 us (0.89)
  waiting for transfers between devices: 79.8 us -> 48.4 us
  Pallas kernels: 153 us -> 123 us
  starting transfers between devices: 14.4 us -> 37.9 us
    all_gather x1, waiting for transfers between devices: 46.7 us -> 22.6 us  [per_device(): lax.all_gather(pack_half(lat_half), ('seq', 'head'), axis=0, tiled=False)]
    all_to_all x1 -> x3, starting transfers between devices: 11.6 us -> 32.2 us  [the longest x1 12 us: gather_by_exchange(): lax.all_to_all(jnp.broadcast_to(x[None], (64,) + x.shape), 'seq', 0, 0, t...]
    pallas_call x1, Pallas kernels: 39.3 us -> 19.4 us  [index_back_call(): pl.pallas_call(functools.partial(index_back_kernel, groups, heads), grid_...]
    pallas_call x1, Pallas kernels: 74.7 us -> 68 us  [attend_call(): pl.pallas_call(functools.partial(attend_kernel, groups, heads), grid_spec...]
    all_to_all x1 -> x3, waiting for transfers between devices: 21.2 us -> 14.5 us  [the longest x1 12.7 us: per_device(): ik_parts = lax.all_to_all(ik_part, 'seq', 0, 0, tiled=True)]
    pallas_call x1, Pallas kernels: 25.9 us -> 22.2 us  [query_grad_call(): pl.pallas_call(functools.partial(query_grad_kernel, 8, heads), in_specs=[...]
    ppermute x6 -> x7, waiting for transfers between devices: 11.8 us -> 11.2 us  [swap_heads(): return lax.ppermute(x, 'head', [(0, 1), (1, 0)])]
    unnamed x13 -> x18, local copies, waits for them, and re-layouts: 22.5 us -> 22.7 us
  transfers between devices with their start and end apart: 11 -> 11, of which waited for: 6 -> 6; matrix products, arithmetic and copies ran while one was open for 14% -> 19% of each run, Pallas kernels for 24% -> 19%
where the time goes in v2:
time: 288 us; the launch traced here: 286 us
  Pallas kernels  123 us (43%)
  waiting for transfers between devices  48.4 us (17%)
  starting transfers between devices  37.9 us (13%)
  other arithmetic  31.1 us (11%)
  local copies, waits for them, and re-layouts  28.3 us (10%)
  between operations  16.9 us (6%)
    pallas_call x1, Pallas kernels, attend_call(): pl.pallas_call(functools.partial(attend_kernel, groups, heads), grid_spec...  68 us
    unnamed x18, local copies, waits for them, and re-layouts  22.7 us
    all_gather x1, waiting for transfers between devices, per_device(): lax.all_gather(pack_half(lat_half), ('seq', 'head'), axis=0, tiled=False)  22.6 us
    pallas_call x1, Pallas kernels, query_grad_call(): pl.pallas_call(functools.partial(query_grad_kernel, 8, heads), in_specs=[...  22.2 us
    pallas_call x1, Pallas kernels, index_back_call(): pl.pallas_call(functools.partial(index_back_kernel, groups, heads), grid_...  19.4 us
    pallas_call x1, Pallas kernels, index_logits_call(): pl.pallas_call(functools.partial(index_logits_kernel, groups, heads), gri...  13.7 us
    all_to_all x1, waiting for transfers between devices, per_device(): ik_parts = lax.all_to_all(ik_part, 'seq', 0, 0, tiled=True)  12.7 us
    all_to_all x1, starting transfers between devices, gather_by_exchange(): lax.all_to_all(jnp.broadcast_to(x[None], (64,) + x.shape), 'seq', 0, 0, t...  12 us
  transfers between devices with their start and end apart: 11, of which 6 were waited for; matrix products, arithmetic and copies ran while one was open for 19% of the time, Pallas kernels for 19%

profile of v2, /device:TPU:1, one launch (start us, length us, event | category | flops | bytes accessed | tf_op | source)
XLA Modules:
  0.0 285.7 jit_solution(8320160157506508441)
XLA Ops:
  7.2 1.0 constant_dynamic-slice_fusion
  10.2 1.2 broadcast_in_dim.22
  11.5 12.0 %all-to-all-start = ((bf16[64,64,128]{2,1,0:T(8,128)(2,1)}), bf16[64,64,128]{2,1,0:T(8,128)(2,1)S(1)}, u32[]{:S(2)}, u32[]{:S(2)}) async-start(bf16[64,64,128]{2,1,0:T(8,128)(2,1)} %broadcast_in_dim.22), calls=%async_computation | async-start | bytes 2097152 | tf_op jit(solution)/shard_map/all_to_all | solution.py:504
  23.4 11.0 %copy.47 = bf16[128,40,576]{2,1,0:T(8,128)(2,1)} copy(bf16[128,40,576]{0,2,1:T(8,128)(2,1)} %param.7) | data formatting | bytes 11796480 | tf_op args[0]
  34.4 11.4 %fusion.2.stk_hbm = bf16[128,80,640]{2,1,0:T(8,128)(2,1)} fusion(bf16[128,40,512]{2,1,0:T(8,128)(2,1)} %param.9, bf16[128,40,576]{2,1,0:T(8,128)(2,1)} %copy.47), kind=kLoop, calls=%fused_computation.4 | loop fusion | flops 52428800 | bytes 24248320 | tf_op jit(solution)/shard_map/concatenate | solution.py:552
  47.3 1.0 collective-permute-start
  54.6 1.5 pad_maximum_fusion
  56.1 13.7 %index_logits.1 = (f32[4096,512]{1,0:T(8,128)}, f32[128,512]{1,0:T(8,128)}) custom-call(s32[512]{0:T(512)} %reshape.85.picks_ref, s32[2]{0:T(128)} %pad_add_fusion.1.own_ref, bf16[4096,128]{1,0:T(8,128)(2,1)} %bitcast.48, f32[32,128]{1,0:T(8,128)} %convert_bitcast_fusion.wt_ref, bf16[128,64,128]{2,1,0:T(8,128)(2,1)} %bitcast.38), custom_call_target="tpu_custom_call" | custom-call | flops 10000000000 | bytes 4000000 | tf_op jit(solution)/shard_map/index_logits/pallas_call | solution.py:397
  69.7 22.6 %all-gather.3.cloned.1.call-done = bf16[36864,128]{1,0:T(8,128)(2,1)} async-done(((bf16[288,128]{1,0:T(8,128)(2,1)}), bf16[36864,128]{1,0:T(8,128)(2,1)}) %all-gather.3.cloned.1.call-update) | async-done | bytes 9437200 | tf_op jit(solution)/shard_map/all_gather | solution.py:544
  92.4 68.0 %attend.1 = (f32[256,40,128]{2,1,0:T(8,128)}, bf16[5120,256]{1,0:T(8,128)(2,1)}, f32[128,512]{1,0:T(8,128)}, bf16[64,288,128]{2,1,0:T(8,128)(2,1)}, bf16[64,288,128]{2,1,0:T(8,128)(2,1)}) custom-call(s32[512]{0:T(512)} %reshape.85.picks_ref, s32[2]{0:T(128)} %pad_add_fusion.1.own_ref, s32[129]{0:T(256)} %pad_add_fusion.tile_ref, ...), custom_call_target="tpu_custom_call" | custom-call | flops 60000002048 | bytes 50000000 | tf_op jit(solution)/shard_map/attend/pallas_call | solution.py:205
  160.9 8.0 %collective-permute-done.2 = bf16[64,288,128]{2,1,0:T(8,128)(2,1)S(1)} collective-permute-done((bf16[64,288,128]{2,1,0:T(8,128)(2,1)}, bf16[64,288,128]{2,1,0:T(8,128)(2,1)S(1)}, u32[]{:S(2)}, u32[]{:S(2)}) %collective-permute-start.2) | collective-permute-done | bytes 4718624 | tf_op jit(solution)/shard_map/ppermute | solution.py:492
  168.9 5.8 %add.89 = bf16[64,288,128]{2,1,0:T(8,128)(2,1)} add(bf16[64,288,128]{2,1,0:T(8,128)(2,1)} %get-tuple-element.29, bf16[64,288,128]{2,1,0:T(8,128)(2,1)S(1)} %collective-permute-done.2) | non-fusion elementwise | flops 2359296 | bytes 14155776 | tf_op jit(solution)/shard_map/add | solution.py:561
  175.0 9.9 %all-to-all-start.1 = ((bf16[64,288,128]{2,1,0:T(8,128)(2,1)}), bf16[64,288,128]{2,1,0:T(8,128)(2,1)}, u32[]{:S(2)}, u32[]{:S(2)}) async-start(bf16[64,288,128]{2,1,0:T(8,128)(2,1)} %add.89), calls=%async_computation.1 | async-start | bytes 9437184 | tf_op jit(solution)/shard_map/all_to_all | solution.py:563
  186.4 19.4 %index_back.1 = (bf16[4096,128]{1,0:T(8,128)(2,1)}, f32[32,128]{1,0:T(8,128)}, bf16[64,128,128]{2,1,0:T(8,128)(2,1)}) custom-call(s32[512]{0:T(512)} %reshape.85.picks_ref, s32[2]{0:T(128)} %pad_add_fusion.1.own_ref, bf16[4096,128]{1,0:T(8,128)(2,1)} %bitcast.49, f32[32,128]{1,0:T(8,128)} %convert_bitcast_fusion.wt_ref, bf16[128,64,128]{2,1,0:T(8,128)(2,1)} %bitcast.39, ...), custom_call_target="tpu_custom_call" | custom-call | flops 20000000000 | bytes 8000000 | tf_op jit(solution)/shard_map/index_back/pallas_call | solution.py:429
  205.8 1.3 dynamic-slice_bitcast_fusion
  208.0 2.3 collective-permute-done.4
  210.2 2.3 bitcast_add_fusion
  212.5 22.2 %query_grad.1 = bf16[5120,640]{1,0:T(8,128)(2,1)} custom-call(s32[2]{0:T(128)} %pad_add_fusion.1.own_ref, s32[129]{0:T(256)} %pad_add_fusion.tile_ref, s32[512]{0:T(512)} %broadcast_add_fusion.pair_ref, f32[256,40,128]{2,1,0:T(8,128)} %get-tuple-element.34.dsx_ref, bf16[5120,256]{1,0:T(8,128)(2,1)} %get-tuple-element.35.dsh_ref, bf16[128,288,128]{2,1,0:T(8,128)(2,1)} %bitcast.47), custom_call_target="tpu_custom_call" | custom-call | flops 12000000000 | bytes 25000000 | tf_op jit(solution)/shard_map/query_grad/pallas_call | solution.py:285
  234.7 10.6 %copy.57 = bf16[128,40,576]{0,2,1:T(8,128)(2,1)} copy(bf16[128,40,576]{2,1,0:T(8,128)(2,1)} %bitcast.35) | data formatting | bytes 11796480
  245.3 1.8 all-to-all-done.1
  247.2 10.3 %all-to-all-start.2 = ((bf16[64,64,128]{2,1,0:T(8,128)(2,1)}), bf16[64,64,128]{2,1,0:T(8,128)(2,1)S(1)}, u32[]{:S(2)}, u32[]{:S(2)}) async-start(bf16[64,64,128]{2,1,0:T(8,128)(2,1)} %bitcast_add_fusion), calls=%async_computation.2 | async-start | bytes 2097152 | tf_op jit(solution)/shard_map/all_to_all | solution.py:577
  257.5 3.0 %reduce_sum.94 = bf16[288,128]{1,0:T(8,128)(2,1)S(1)} reduce(bf16[64,288,128]{2,1,0:T(8,128)(2,1)} %all-to-all-done.1, bf16[]{:T(256)} %constant.75.clone.1), dimensions={0}, to_apply=%region_7.8 | reduce | flops 2322432 | bytes 4792322 | tf_op jit(solution)/shard_map/reduce_sum | solution.py:500
  262.3 12.7 %all-to-all-done.2 = bf16[64,64,128]{2,1,0:T(8,128)(2,1)S(1)} async-done(((bf16[64,64,128]{2,1,0:T(8,128)(2,1)}), bf16[64,64,128]{2,1,0:T(8,128)(2,1)S(1)}, u32[]{:S(2)}, u32[]{:S(2)}) %all-to-all-start.2) | async-done | bytes 1048608 | tf_op jit(solution)/shard_map/all_to_all | solution.py:577
  275.2 2.2 collective-permute-start.6
  (66 shorter events, 13.6 us)
Async XLA Ops:
  7.2 3.0 %copy-start = (bf16[128,128]{1,0:T(8,128)(2,1)S(1)}, bf16[128,128]{1,0:T(8,128)(2,1)}, u32[]{:S(2)}) copy-start(bf16[128,128]{1,0:T(8,128)(2,1)} %param.12) | copy-start | bytes 98308
  7.2 85.2 %all-gather.3.cloned.1.call-start = ((), (), s32[]{:S(2)}) async-start(), calls=%async_computation.3 | async-start | bytes 9510912 | tf_op jit(solution)/shard_map/all_gather | solution.py:544
  11.5 35.8 %all-to-all-start = ((bf16[64,64,128]{2,1,0:T(8,128)(2,1)}), bf16[64,64,128]{2,1,0:T(8,128)(2,1)S(1)}, u32[]{:S(2)}, u32[]{:S(2)}) async-start(bf16[64,64,128]{2,1,0:T(8,128)(2,1)} %broadcast_in_dim.22), calls=%async_computation | async-start | bytes 2097152 | tf_op jit(solution)/shard_map/all_to_all | solution.py:504
  34.4 11.4 %copy-start.5 = (s32[128,4]{0,1:T(4,128)S(1)}, s32[128,4]{0,1:T(4,128)}, u32[]{:S(2)}) copy-start(s32[128,4]{0,1:T(4,128)} %param.13) | copy-start | bytes 6148
  34.4 19.4 %copy-start.4 = (bf16[128,32]{0,1:T(8,128)(2,1)S(1)}, bf16[128,32]{0,1:T(8,128)(2,1)}, u32[]{:S(2)}) copy-start(bf16[128,32]{0,1:T(8,128)(2,1)} %param.11) | copy-start | bytes 24580
  47.3 7.1 %collective-permute-start = (bf16[64,64,128]{2,1,0:T(8,128)(2,1)S(1)}, bf16[64,64,128]{2,1,0:T(8,128)(2,1)S(1)}, u32[]{:S(2)}, u32[]{:S(2)}) collective-permute-start(bf16[64,64,128]{2,1,0:T(8,128)(2,1)S(1)} %all-to-all-done), channel_id=1, source_target_pairs={{0,1},{1,0},{2,3},{3,2},{4,5},{5,4},{6,7},{7,6},{8,9},{9,8},{10,11... | collective-permute-start | bytes 3145736 | tf_op jit(solution)/shard_map/ppermute | solution.py:492
  92.4 68.3 %copy-start.2 = (f32[128,512]{1,0:T(8,128)S(1)}, f32[128,512]{1,0:T(8,128)}, u32[]{:S(2)}) copy-start(f32[128,512]{1,0:T(8,128)} %get-tuple-element.26) | copy-start | bytes 786436
  160.3 8.6 %collective-permute-start.2 = (bf16[64,288,128]{2,1,0:T(8,128)(2,1)}, bf16[64,288,128]{2,1,0:T(8,128)(2,1)S(1)}, u32[]{:S(2)}, u32[]{:S(2)}) collective-permute-start(bf16[64,288,128]{2,1,0:T(8,128)(2,1)} %get-tuple-element.30), channel_id=1, source_target_pairs={{0,1},{1,0},{2,3},{3,2},{4,5},{5,4},{6,7},{7,6},{8,9},{9,8},{10,11... | collective-permute-start | bytes 14155784 | tf_op jit(solution)/shard_map/ppermute | solution.py:492
  160.7 24.2 %collective-permute-start.1 = (f32[128,512]{1,0:T(8,128)S(1)}, f32[128,512]{1,0:T(8,128)S(1)}, u32[]{:S(2)}, u32[]{:S(2)}) collective-permute-start(f32[128,512]{1,0:T(8,128)S(1)} %copy-done.2), channel_id=1, source_target_pairs={{0,1},{1,0},{2,3},{3,2},{4,5},{5,4},{6,7},{7,6},{8,9},{9,8},{10,11... | collective-permute-start | bytes 786440 | tf_op jit(solution)/shard_map/ppermute | solution.py:492
  168.9 5.8 %copy-start.3 = (f32[128,512]{1,0:T(8,128)S(1)}, f32[128,512]{1,0:T(8,128)}, u32[]{:S(2)}) copy-start(f32[128,512]{1,0:T(8,128)} %get-tuple-element.31) | copy-start | bytes 786436
  174.7 10.9 %collective-permute-start.3 = (f32[128,512]{1,0:T(8,128)S(1)}, f32[128,512]{1,0:T(8,128)S(1)}, u32[]{:S(2)}, u32[]{:S(2)}) collective-permute-start(f32[128,512]{1,0:T(8,128)S(1)} %copy-done.3), channel_id=1, source_target_pairs={{0,1},{1,0},{2,3},{3,2},{4,5},{5,4},{6,7},{7,6},{8,9},{9,8},{10,11... | collective-permute-start | bytes 786440 | tf_op jit(solution)/shard_map/ppermute | solution.py:492
  175.0 72.1 %all-to-all-start.1 = ((bf16[64,288,128]{2,1,0:T(8,128)(2,1)}), bf16[64,288,128]{2,1,0:T(8,128)(2,1)}, u32[]{:S(2)}, u32[]{:S(2)}) async-start(bf16[64,288,128]{2,1,0:T(8,128)(2,1)} %add.89), calls=%async_computation.1 | async-start | bytes 9437184 | tf_op jit(solution)/shard_map/all_to_all | solution.py:563
  207.2 3.1 %collective-permute-start.4 = (bf16[64,64,128]{2,1,0:T(8,128)(2,1)S(1)}, bf16[64,64,128]{2,1,0:T(8,128)(2,1)S(1)}, u32[]{:S(2)}, u32[]{:S(2)}) collective-permute-start(bf16[64,64,128]{2,1,0:T(8,128)(2,1)S(1)} %dynamic-slice_bitcast_fusion), channel_id=1, source_target_pairs={{0,1},{1,0},{2,3},{3,2},{4,5},{5,4},{6,7},{7,6},{8,9},{9,8},{10,11... | collective-permute-start | bytes 3145736 | tf_op jit(solution)/shard_map/ppermute | solution.py:492
  234.7 44.2 %copy-start.1 = (bf16[128,128]{1,0:T(8,128)(2,1)S(1)}, bf16[128,128]{1,0:T(8,128)(2,1)}, u32[]{:S(2)}) copy-start(bf16[128,128]{1,0:T(8,128)(2,1)} %param.12) | copy-start | bytes 98308
  247.2 27.9 %all-to-all-start.2 = ((bf16[64,64,128]{2,1,0:T(8,128)(2,1)}), bf16[64,64,128]{2,1,0:T(8,128)(2,1)S(1)}, u32[]{:S(2)}, u32[]{:S(2)}) async-start(bf16[64,64,128]{2,1,0:T(8,128)(2,1)} %bitcast_add_fusion), calls=%async_computation.2 | async-start | bytes 2097152 | tf_op jit(solution)/shard_map/all_to_all | solution.py:577
  260.6 1.6 collective-permute-start.5
  275.2 3.1 %collective-permute-start.6 = (bf16[64,128]{1,0:T(8,128)(2,1)S(1)}, bf16[64,128]{1,0:T(8,128)(2,1)S(1)}, u32[]{:S(2)}, u32[]{:S(2)}) collective-permute-start(bf16[64,128]{1,0:T(8,128)(2,1)S(1)} %reduce_sum.95), channel_id=1, source_target_pairs={{0,1},{1,0},{2,3},{3,2},{4,5},{5,4},{6,7},{7,6},{8,9},{9,8},{10,11... | collective-permute-start | bytes 49160 | tf_op jit(solution)/shard_map/ppermute | solution.py:492
Sparse Core Ops, SparseCore 0:
  11.6 80.7 all-gather.2

commit v3 on v2

--- a/solution.py
+++ b/solution.py
@@ -18,12 +18,12 @@
 neg_large = -1e30
 inv_root = IH ** (-0.5)
 
-G_ATT = 8
+G_ATT = 16
 G_IDX = 8
 UNROLL = 4
 PAIRS = 4
 HALF = BLOCK // 2
-VMEM_LIMIT = 58 * 1024 * 1024
+VMEM_LIMIT = 60 * 1024 * 1024
 
 
 def dot(a, b, ca, cb):

time: 288 us -> 284 us (0.986)
  Pallas kernels: 123 us -> 119 us
    pallas_call x1, Pallas kernels: 68 us -> 64.1 us  [attend_call(): pl.pallas_call(functools.partial(attend_kernel, groups, heads), grid_spec...]
  transfers between devices with their start and end apart: 11 -> 11, of which waited for: 6 -> 6; matrix products, arithmetic and copies ran while one was open for 19% -> 20% of each run, Pallas kernels for 19% -> 20%
where the time goes in v3:
time: 284 us; the launch traced here: 282 us
  Pallas kernels  119 us (42%)
  waiting for transfers between devices  48 us (17%)
  starting transfers between devices  38.1 us (13%)
  other arithmetic  31.1 us (11%)
  local copies, waits for them, and re-layouts  28.3 us (10%)
  between operations  16.9 us (6%)
    pallas_call x1, Pallas kernels, attend_call(): pl.pallas_call(functools.partial(attend_kernel, groups, heads), grid_spec...  64.1 us
    unnamed x18, local copies, waits for them, and re-layouts  22.7 us
    all_gather x1, waiting for transfers between devices, per_device(): lax.all_gather(pack_half(lat_half), ('seq', 'head'), axis=0, tiled=False)  22.6 us
    pallas_call x1, Pallas kernels, query_grad_call(): pl.pallas_call(functools.partial(query_grad_kernel, 8, heads), in_specs=[...  22.2 us
    pallas_call x1, Pallas kernels, index_back_call(): pl.pallas_call(functools.partial(index_back_kernel, groups, heads), grid_...  19.4 us
    pallas_call x1, Pallas kernels, index_logits_call(): pl.pallas_call(functools.partial(index_logits_kernel, groups, heads), gri...  13.7 us
    all_to_all x1, waiting for transfers between devices, per_device(): ik_parts = lax.all_to_all(ik_part, 'seq', 0, 0, tiled=True)  12.6 us
    all_to_all x1, starting transfers between devices, gather_by_exchange(): lax.all_to_all(jnp.broadcast_to(x[None], (64,) + x.shape), 'seq', 0, 0, t...  12 us
  transfers between devices with their start and end apart: 11, of which 6 were waited for; matrix products, arithmetic and copies ran while one was open for 20% of the time, Pallas kernels for 20%

profile of v3, /device:TPU:1, one launch (start us, length us, event | category | flops | bytes accessed | tf_op | source)
XLA Modules:
  0.0 281.7 jit_solution(16912155682478308452)
XLA Ops:
  7.2 1.0 constant_dynamic-slice_fusion
  10.2 1.2 broadcast_in_dim.22
  11.5 12.0 %all-to-all-start = ((bf16[64,64,128]{2,1,0:T(8,128)(2,1)}), bf16[64,64,128]{2,1,0:T(8,128)(2,1)S(1)}, u32[]{:S(2)}, u32[]{:S(2)}) async-start(bf16[64,64,128]{2,1,0:T(8,128)(2,1)} %broadcast_in_dim.22), calls=%async_computation | async-start | bytes 2097152 | tf_op jit(solution)/shard_map/all_to_all | solution.py:504
  23.4 11.0 %copy.47 = bf16[128,40,576]{2,1,0:T(8,128)(2,1)} copy(bf16[128,40,576]{0,2,1:T(8,128)(2,1)} %param.7) | data formatting | bytes 11796480 | tf_op args[0]
  34.4 11.4 %fusion.2.stk_hbm = bf16[128,80,640]{2,1,0:T(8,128)(2,1)} fusion(bf16[128,40,512]{2,1,0:T(8,128)(2,1)} %param.9, bf16[128,40,576]{2,1,0:T(8,128)(2,1)} %copy.47), kind=kLoop, calls=%fused_computation.4 | loop fusion | flops 52428800 | bytes 24248320 | tf_op jit(solution)/shard_map/concatenate | solution.py:552
  47.3 1.0 collective-permute-start
  54.6 1.5 pad_maximum_fusion
  56.1 13.7 %index_logits.1 = (f32[4096,512]{1,0:T(8,128)}, f32[128,512]{1,0:T(8,128)}) custom-call(s32[512]{0:T(512)} %reshape.85.picks_ref, s32[2]{0:T(128)} %pad_add_fusion.1.own_ref, bf16[4096,128]{1,0:T(8,128)(2,1)} %bitcast.48, f32[32,128]{1,0:T(8,128)} %convert_bitcast_fusion.wt_ref, bf16[128,64,128]{2,1,0:T(8,128)(2,1)} %bitcast.38), custom_call_target="tpu_custom_call" | custom-call | flops 10000000000 | bytes 4000000 | tf_op jit(solution)/shard_map/index_logits/pallas_call | solution.py:397
  69.7 22.6 %all-gather.3.cloned.1.call-done = bf16[36864,128]{1,0:T(8,128)(2,1)} async-done(((bf16[288,128]{1,0:T(8,128)(2,1)}), bf16[36864,128]{1,0:T(8,128)(2,1)}) %all-gather.3.cloned.1.call-update) | async-done | bytes 9437200 | tf_op jit(solution)/shard_map/all_gather | solution.py:544
  92.4 64.1 %attend.1 = (f32[256,40,128]{2,1,0:T(8,128)}, bf16[5120,256]{1,0:T(8,128)(2,1)}, f32[128,512]{1,0:T(8,128)}, bf16[64,288,128]{2,1,0:T(8,128)(2,1)}, bf16[64,288,128]{2,1,0:T(8,128)(2,1)}) custom-call(s32[512]{0:T(512)} %reshape.85.picks_ref, s32[2]{0:T(128)} %pad_add_fusion.1.own_ref, s32[129]{0:T(256)} %pad_add_fusion.tile_ref, ...), custom_call_target="tpu_custom_call" | custom-call | flops 60000002048 | bytes 50000000 | tf_op jit(solution)/shard_map/attend/pallas_call | solution.py:205
  157.1 8.0 %collective-permute-done.2 = bf16[64,288,128]{2,1,0:T(8,128)(2,1)S(1)} collective-permute-done((bf16[64,288,128]{2,1,0:T(8,128)(2,1)}, bf16[64,288,128]{2,1,0:T(8,128)(2,1)S(1)}, u32[]{:S(2)}, u32[]{:S(2)}) %collective-permute-start.2) | collective-permute-done | bytes 4718624 | tf_op jit(solution)/shard_map/ppermute | solution.py:492
  165.1 5.8 %add.89 = bf16[64,288,128]{2,1,0:T(8,128)(2,1)} add(bf16[64,288,128]{2,1,0:T(8,128)(2,1)} %get-tuple-element.29, bf16[64,288,128]{2,1,0:T(8,128)(2,1)S(1)} %collective-permute-done.2) | non-fusion elementwise | flops 2359296 | bytes 14155776 | tf_op jit(solution)/shard_map/add | solution.py:561
  171.2 9.9 %all-to-all-start.1 = ((bf16[64,288,128]{2,1,0:T(8,128)(2,1)}), bf16[64,288,128]{2,1,0:T(8,128)(2,1)}, u32[]{:S(2)}, u32[]{:S(2)}) async-start(bf16[64,288,128]{2,1,0:T(8,128)(2,1)} %add.89), calls=%async_computation.1 | async-start | bytes 9437184 | tf_op jit(solution)/shard_map/all_to_all | solution.py:563
  182.6 19.4 %index_back.1 = (bf16[4096,128]{1,0:T(8,128)(2,1)}, f32[32,128]{1,0:T(8,128)}, bf16[64,128,128]{2,1,0:T(8,128)(2,1)}) custom-call(s32[512]{0:T(512)} %reshape.85.picks_ref, s32[2]{0:T(128)} %pad_add_fusion.1.own_ref, bf16[4096,128]{1,0:T(8,128)(2,1)} %bitcast.49, f32[32,128]{1,0:T(8,128)} %convert_bitcast_fusion.wt_ref, bf16[128,64,128]{2,1,0:T(8,128)(2,1)} %bitcast.39, ...), custom_call_target="tpu_custom_call" | custom-call | flops 20000000000 | bytes 8000000 | tf_op jit(solution)/shard_map/index_back/pallas_call | solution.py:429
  202.0 1.3 dynamic-slice_bitcast_fusion
  204.0 2.3 collective-permute-done.4
  206.2 2.3 bitcast_add_fusion
  208.5 22.2 %query_grad.1 = bf16[5120,640]{1,0:T(8,128)(2,1)} custom-call(s32[2]{0:T(128)} %pad_add_fusion.1.own_ref, s32[129]{0:T(256)} %pad_add_fusion.tile_ref, s32[512]{0:T(512)} %broadcast_add_fusion.pair_ref, f32[256,40,128]{2,1,0:T(8,128)} %get-tuple-element.34.dsx_ref, bf16[5120,256]{1,0:T(8,128)(2,1)} %get-tuple-element.35.dsh_ref, bf16[128,288,128]{2,1,0:T(8,128)(2,1)} %bitcast.47), custom_call_target="tpu_custom_call" | custom-call | flops 12000000000 | bytes 25000000 | tf_op jit(solution)/shard_map/query_grad/pallas_call | solution.py:285
  230.7 10.6 %copy.57 = bf16[128,40,576]{0,2,1:T(8,128)(2,1)} copy(bf16[128,40,576]{2,1,0:T(8,128)(2,1)} %bitcast.35) | data formatting | bytes 11796480
  241.3 1.5 all-to-all-done.1
  242.8 10.6 %all-to-all-start.2 = ((bf16[64,64,128]{2,1,0:T(8,128)(2,1)}), bf16[64,64,128]{2,1,0:T(8,128)(2,1)S(1)}, u32[]{:S(2)}, u32[]{:S(2)}) async-start(bf16[64,64,128]{2,1,0:T(8,128)(2,1)} %bitcast_add_fusion), calls=%async_computation.2 | async-start | bytes 2097152 | tf_op jit(solution)/shard_map/all_to_all | solution.py:577
  253.5 3.0 %reduce_sum.94 = bf16[288,128]{1,0:T(8,128)(2,1)S(1)} reduce(bf16[64,288,128]{2,1,0:T(8,128)(2,1)} %all-to-all-done.1, bf16[]{:T(256)} %constant.75.clone.1), dimensions={0}, to_apply=%region_7.8 | reduce | flops 2322432 | bytes 4792322 | tf_op jit(solution)/shard_map/reduce_sum | solution.py:500
  258.3 12.6 %all-to-all-done.2 = bf16[64,64,128]{2,1,0:T(8,128)(2,1)S(1)} async-done(((bf16[64,64,128]{2,1,0:T(8,128)(2,1)}), bf16[64,64,128]{2,1,0:T(8,128)(2,1)S(1)}, u32[]{:S(2)}, u32[]{:S(2)}) %all-to-all-start.2) | async-done | bytes 1048608 | tf_op jit(solution)/shard_map/all_to_all | solution.py:577
  271.1 2.3 collective-permute-start.6
  (66 shorter events, 13.5 us)
Async XLA Ops:
  7.2 3.0 %copy-start = (bf16[128,128]{1,0:T(8,128)(2,1)S(1)}, bf16[128,128]{1,0:T(8,128)(2,1)}, u32[]{:S(2)}) copy-start(bf16[128,128]{1,0:T(8,128)(2,1)} %param.12) | copy-start | bytes 98308
  7.2 85.2 %all-gather.3.cloned.1.call-start = ((), (), s32[]{:S(2)}) async-start(), calls=%async_computation.3 | async-start | bytes 9510912 | tf_op jit(solution)/shard_map/all_gather | solution.py:544
  11.5 35.8 %all-to-all-start = ((bf16[64,64,128]{2,1,0:T(8,128)(2,1)}), bf16[64,64,128]{2,1,0:T(8,128)(2,1)S(1)}, u32[]{:S(2)}, u32[]{:S(2)}) async-start(bf16[64,64,128]{2,1,0:T(8,128)(2,1)} %broadcast_in_dim.22), calls=%async_computation | async-start | bytes 2097152 | tf_op jit(solution)/shard_map/all_to_all | solution.py:504
  34.4 11.4 %copy-start.5 = (s32[128,4]{0,1:T(4,128)S(1)}, s32[128,4]{0,1:T(4,128)}, u32[]{:S(2)}) copy-start(s32[128,4]{0,1:T(4,128)} %param.13) | copy-start | bytes 6148
  34.4 19.4 %copy-start.4 = (bf16[128,32]{0,1:T(8,128)(2,1)S(1)}, bf16[128,32]{0,1:T(8,128)(2,1)}, u32[]{:S(2)}) copy-start(bf16[128,32]{0,1:T(8,128)(2,1)} %param.11) | copy-start | bytes 24580
  47.3 7.1 %collective-permute-start = (bf16[64,64,128]{2,1,0:T(8,128)(2,1)S(1)}, bf16[64,64,128]{2,1,0:T(8,128)(2,1)S(1)}, u32[]{:S(2)}, u32[]{:S(2)}) collective-permute-start(bf16[64,64,128]{2,1,0:T(8,128)(2,1)S(1)} %all-to-all-done), channel_id=1, source_target_pairs={{0,1},{1,0},{2,3},{3,2},{4,5},{5,4},{6,7},{7,6},{8,9},{9,8},{10,11... | collective-permute-start | bytes 3145736 | tf_op jit(solution)/shard_map/ppermute | solution.py:492
  92.4 64.5 %copy-start.2 = (f32[128,512]{1,0:T(8,128)S(1)}, f32[128,512]{1,0:T(8,128)}, u32[]{:S(2)}) copy-start(f32[128,512]{1,0:T(8,128)} %get-tuple-element.26) | copy-start | bytes 786436
  156.5 8.6 %collective-permute-start.2 = (bf16[64,288,128]{2,1,0:T(8,128)(2,1)}, bf16[64,288,128]{2,1,0:T(8,128)(2,1)S(1)}, u32[]{:S(2)}, u32[]{:S(2)}) collective-permute-start(bf16[64,288,128]{2,1,0:T(8,128)(2,1)} %get-tuple-element.30), channel_id=1, source_target_pairs={{0,1},{1,0},{2,3},{3,2},{4,5},{5,4},{6,7},{7,6},{8,9},{9,8},{10,11... | collective-permute-start | bytes 14155784 | tf_op jit(solution)/shard_map/ppermute | solution.py:492
  156.8 24.2 %collective-permute-start.1 = (f32[128,512]{1,0:T(8,128)S(1)}, f32[128,512]{1,0:T(8,128)S(1)}, u32[]{:S(2)}, u32[]{:S(2)}) collective-permute-start(f32[128,512]{1,0:T(8,128)S(1)} %copy-done.2), channel_id=1, source_target_pairs={{0,1},{1,0},{2,3},{3,2},{4,5},{5,4},{6,7},{7,6},{8,9},{9,8},{10,11... | collective-permute-start | bytes 786440 | tf_op jit(solution)/shard_map/ppermute | solution.py:492
  165.1 5.8 %copy-start.3 = (f32[128,512]{1,0:T(8,128)S(1)}, f32[128,512]{1,0:T(8,128)}, u32[]{:S(2)}) copy-start(f32[128,512]{1,0:T(8,128)} %get-tuple-element.31) | copy-start | bytes 786436
  170.9 10.9 %collective-permute-start.3 = (f32[128,512]{1,0:T(8,128)S(1)}, f32[128,512]{1,0:T(8,128)S(1)}, u32[]{:S(2)}, u32[]{:S(2)}) collective-permute-start(f32[128,512]{1,0:T(8,128)S(1)} %copy-done.3), channel_id=1, source_target_pairs={{0,1},{1,0},{2,3},{3,2},{4,5},{5,4},{6,7},{7,6},{8,9},{9,8},{10,11... | collective-permute-start | bytes 786440 | tf_op jit(solution)/shard_map/ppermute | solution.py:492
  171.2 71.7 %all-to-all-start.1 = ((bf16[64,288,128]{2,1,0:T(8,128)(2,1)}), bf16[64,288,128]{2,1,0:T(8,128)(2,1)}, u32[]{:S(2)}, u32[]{:S(2)}) async-start(bf16[64,288,128]{2,1,0:T(8,128)(2,1)} %add.89), calls=%async_computation.1 | async-start | bytes 9437184 | tf_op jit(solution)/shard_map/all_to_all | solution.py:563
  203.3 2.9 %collective-permute-start.4 = (bf16[64,64,128]{2,1,0:T(8,128)(2,1)S(1)}, bf16[64,64,128]{2,1,0:T(8,128)(2,1)S(1)}, u32[]{:S(2)}, u32[]{:S(2)}) collective-permute-start(bf16[64,64,128]{2,1,0:T(8,128)(2,1)S(1)} %dynamic-slice_bitcast_fusion), channel_id=1, source_target_pairs={{0,1},{1,0},{2,3},{3,2},{4,5},{5,4},{6,7},{7,6},{8,9},{9,8},{10,11... | collective-permute-start | bytes 3145736 | tf_op jit(solution)/shard_map/ppermute | solution.py:492
  230.7 44.1 %copy-start.1 = (bf16[128,128]{1,0:T(8,128)(2,1)S(1)}, bf16[128,128]{1,0:T(8,128)(2,1)}, u32[]{:S(2)}) copy-start(bf16[128,128]{1,0:T(8,128)(2,1)} %param.12) | copy-start | bytes 98308
  242.8 28.1 %all-to-all-start.2 = ((bf16[64,64,128]{2,1,0:T(8,128)(2,1)}), bf16[64,64,128]{2,1,0:T(8,128)(2,1)S(1)}, u32[]{:S(2)}, u32[]{:S(2)}) async-start(bf16[64,64,128]{2,1,0:T(8,128)(2,1)} %bitcast_add_fusion), calls=%async_computation.2 | async-start | bytes 2097152 | tf_op jit(solution)/shard_map/all_to_all | solution.py:577
  256.6 1.7 collective-permute-start.5
  271.1 3.1 %collective-permute-start.6 = (bf16[64,128]{1,0:T(8,128)(2,1)S(1)}, bf16[64,128]{1,0:T(8,128)(2,1)S(1)}, u32[]{:S(2)}, u32[]{:S(2)}) collective-permute-start(bf16[64,128]{1,0:T(8,128)(2,1)S(1)} %reduce_sum.95), channel_id=1, source_target_pairs={{0,1},{1,0},{2,3},{3,2},{4,5},{5,4},{6,7},{7,6},{8,9},{9,8},{10,11... | collective-permute-start | bytes 49160 | tf_op jit(solution)/shard_map/ppermute | solution.py:492
Sparse Core Ops, SparseCore 0:
  11.6 80.7 all-gather.2

commit v4 on v3

--- a/solution.py
+++ b/solution.py
@@ -20,7 +20,7 @@
 
 G_ATT = 16
 G_IDX = 8
-UNROLL = 4
+UNROLL = 8
 PAIRS = 4
 HALF = BLOCK // 2
 VMEM_LIMIT = 60 * 1024 * 1024

time: 284 us -> 281 us (0.989)
  transfers between devices with their start and end apart: 11 -> 11, of which waited for: 6 -> 6; matrix products, arithmetic and copies ran while one was open for 20% -> 20% of each run, Pallas kernels for 20% -> 19%
where the time goes in v4:
time: 281 us; the launch traced here: 279 us
  Pallas kernels  117 us (42%)
  waiting for transfers between devices  48.2 us (17%)
  starting transfers between devices  36.9 us (13%)
  other arithmetic  31.1 us (11%)
  local copies, waits for them, and re-layouts  28.3 us (10%)
  between operations  16.9 us (6%)
    pallas_call x1, Pallas kernels, attend_call(): pl.pallas_call(functools.partial(attend_kernel, groups, heads), grid_spec...  62.9 us
    unnamed x18, local copies, waits for them, and re-layouts  22.7 us
    all_gather x1, waiting for transfers between devices, per_device(): lax.all_gather(pack_half(lat_half), ('seq', 'head'), axis=0, tiled=False)  22.6 us
    pallas_call x1, Pallas kernels, query_grad_call(): pl.pallas_call(functools.partial(query_grad_kernel, 8, heads), in_specs=[...  21.2 us
    pallas_call x1, Pallas kernels, index_back_call(): pl.pallas_call(functools.partial(index_back_kernel, groups, heads), grid_...  19.4 us
    pallas_call x1, Pallas kernels, index_logits_call(): pl.pallas_call(functools.partial(index_logits_kernel, groups, heads), gri...  13.7 us
    all_to_all x1, starting transfers between devices, gather_by_exchange(): lax.all_to_all(jnp.broadcast_to(x[None], (64,) + x.shape), 'seq', 0, 0, t...  12 us
    all_to_all x1, waiting for transfers between devices, per_device(): ik_parts = lax.all_to_all(ik_part, 'seq', 0, 0, tiled=True)  11.8 us
  transfers between devices with their start and end apart: 11, of which 6 were waited for; matrix products, arithmetic and copies ran while one was open for 20% of the time, Pallas kernels for 19%

profile of v4, /device:TPU:1, one launch (start us, length us, event | category | flops | bytes accessed | tf_op | source)
XLA Modules:
  0.0 278.5 jit_solution(12068024216167437020)
XLA Ops:
  10.2 1.2 broadcast_in_dim.22
  11.5 12.0 %all-to-all-start = ((bf16[64,64,128]{2,1,0:T(8,128)(2,1)}), bf16[64,64,128]{2,1,0:T(8,128)(2,1)S(1)}, u32[]{:S(2)}, u32[]{:S(2)}) async-start(bf16[64,64,128]{2,1,0:T(8,128)(2,1)} %broadcast_in_dim.22), calls=%async_computation | async-start | bytes 2097152 | tf_op jit(solution)/shard_map/all_to_all | solution.py:504
  23.4 11.0 %copy.47 = bf16[128,40,576]{2,1,0:T(8,128)(2,1)} copy(bf16[128,40,576]{0,2,1:T(8,128)(2,1)} %param.7) | data formatting | bytes 11796480 | tf_op args[0]
  34.4 11.4 %fusion.2.stk_hbm = bf16[128,80,640]{2,1,0:T(8,128)(2,1)} fusion(bf16[128,40,512]{2,1,0:T(8,128)(2,1)} %param.9, bf16[128,40,576]{2,1,0:T(8,128)(2,1)} %copy.47), kind=kLoop, calls=%fused_computation.4 | loop fusion | flops 52428800 | bytes 24248320 | tf_op jit(solution)/shard_map/concatenate | solution.py:552
  47.3 1.0 collective-permute-start
  54.6 1.5 pad_maximum_fusion
  56.1 13.7 %index_logits.1 = (f32[4096,512]{1,0:T(8,128)}, f32[128,512]{1,0:T(8,128)}) custom-call(s32[512]{0:T(512)} %reshape.85.picks_ref, s32[2]{0:T(128)} %pad_add_fusion.1.own_ref, bf16[4096,128]{1,0:T(8,128)(2,1)} %bitcast.48, f32[32,128]{1,0:T(8,128)} %convert_bitcast_fusion.wt_ref, bf16[128,64,128]{2,1,0:T(8,128)(2,1)} %bitcast.38), custom_call_target="tpu_custom_call" | custom-call | flops 10000000000 | bytes 4000000 | tf_op jit(solution)/shard_map/index_logits/pallas_call | solution.py:397
  69.7 22.6 %all-gather.3.cloned.1.call-done = bf16[36864,128]{1,0:T(8,128)(2,1)} async-done(((bf16[288,128]{1,0:T(8,128)(2,1)}), bf16[36864,128]{1,0:T(8,128)(2,1)}) %all-gather.3.cloned.1.call-update) | async-done | bytes 9437200 | tf_op jit(solution)/shard_map/all_gather | solution.py:544
  92.4 62.9 %attend.1 = (f32[256,40,128]{2,1,0:T(8,128)}, bf16[5120,256]{1,0:T(8,128)(2,1)}, f32[128,512]{1,0:T(8,128)}, bf16[64,288,128]{2,1,0:T(8,128)(2,1)}, bf16[64,288,128]{2,1,0:T(8,128)(2,1)}) custom-call(s32[512]{0:T(512)} %reshape.85.picks_ref, s32[2]{0:T(128)} %pad_add_fusion.1.own_ref, s32[129]{0:T(256)} %pad_add_fusion.tile_ref, ...), custom_call_target="tpu_custom_call" | custom-call | flops 60000002048 | bytes 50000000 | tf_op jit(solution)/shard_map/attend/pallas_call | solution.py:205
  155.9 8.0 %collective-permute-done.2 = bf16[64,288,128]{2,1,0:T(8,128)(2,1)S(1)} collective-permute-done((bf16[64,288,128]{2,1,0:T(8,128)(2,1)}, bf16[64,288,128]{2,1,0:T(8,128)(2,1)S(1)}, u32[]{:S(2)}, u32[]{:S(2)}) %collective-permute-start.2) | collective-permute-done | bytes 4718624 | tf_op jit(solution)/shard_map/ppermute | solution.py:492
  163.9 5.8 %add.89 = bf16[64,288,128]{2,1,0:T(8,128)(2,1)} add(bf16[64,288,128]{2,1,0:T(8,128)(2,1)} %get-tuple-element.29, bf16[64,288,128]{2,1,0:T(8,128)(2,1)S(1)} %collective-permute-done.2) | non-fusion elementwise | flops 2359296 | bytes 14155776 | tf_op jit(solution)/shard_map/add | solution.py:561
  169.9 9.3 %all-to-all-start.1 = ((bf16[64,288,128]{2,1,0:T(8,128)(2,1)}), bf16[64,288,128]{2,1,0:T(8,128)(2,1)}, u32[]{:S(2)}, u32[]{:S(2)}) async-start(bf16[64,288,128]{2,1,0:T(8,128)(2,1)} %add.89), calls=%async_computation.1 | async-start | bytes 9437184 | tf_op jit(solution)/shard_map/all_to_all | solution.py:563
  180.8 19.4 %index_back.1 = (bf16[4096,128]{1,0:T(8,128)(2,1)}, f32[32,128]{1,0:T(8,128)}, bf16[64,128,128]{2,1,0:T(8,128)(2,1)}) custom-call(s32[512]{0:T(512)} %reshape.85.picks_ref, s32[2]{0:T(128)} %pad_add_fusion.1.own_ref, bf16[4096,128]{1,0:T(8,128)(2,1)} %bitcast.49, f32[32,128]{1,0:T(8,128)} %convert_bitcast_fusion.wt_ref, bf16[128,64,128]{2,1,0:T(8,128)(2,1)} %bitcast.39, ...), custom_call_target="tpu_custom_call" | custom-call | flops 20000000000 | bytes 8000000 | tf_op jit(solution)/shard_map/index_back/pallas_call | solution.py:429
  200.2 1.3 dynamic-slice_bitcast_fusion
  202.2 2.3 collective-permute-done.4
  204.4 2.3 bitcast_add_fusion
  206.7 21.2 %query_grad.1 = bf16[5120,640]{1,0:T(8,128)(2,1)} custom-call(s32[2]{0:T(128)} %pad_add_fusion.1.own_ref, s32[129]{0:T(256)} %pad_add_fusion.tile_ref, s32[512]{0:T(512)} %broadcast_add_fusion.pair_ref, f32[256,40,128]{2,1,0:T(8,128)} %get-tuple-element.34.dsx_ref, bf16[5120,256]{1,0:T(8,128)(2,1)} %get-tuple-element.35.dsh_ref, bf16[128,288,128]{2,1,0:T(8,128)(2,1)} %bitcast.47), custom_call_target="tpu_custom_call" | custom-call | flops 12000000000 | bytes 25000000 | tf_op jit(solution)/shard_map/query_grad/pallas_call | solution.py:285
  227.9 10.6 %copy.57 = bf16[128,40,576]{0,2,1:T(8,128)(2,1)} copy(bf16[128,40,576]{2,1,0:T(8,128)(2,1)} %bitcast.35) | data formatting | bytes 11796480
  238.5 2.5 all-to-all-done.1
  241.0 9.3 %all-to-all-start.2 = ((bf16[64,64,128]{2,1,0:T(8,128)(2,1)}), bf16[64,64,128]{2,1,0:T(8,128)(2,1)S(1)}, u32[]{:S(2)}, u32[]{:S(2)}) async-start(bf16[64,64,128]{2,1,0:T(8,128)(2,1)} %bitcast_add_fusion), calls=%async_computation.2 | async-start | bytes 2097152 | tf_op jit(solution)/shard_map/all_to_all | solution.py:577
  250.3 3.0 %reduce_sum.94 = bf16[288,128]{1,0:T(8,128)(2,1)S(1)} reduce(bf16[64,288,128]{2,1,0:T(8,128)(2,1)} %all-to-all-done.1, bf16[]{:T(256)} %constant.78.clone.1), dimensions={0}, to_apply=%region_7.8 | reduce | flops 2322432 | bytes 4792322 | tf_op jit(solution)/shard_map/reduce_sum | solution.py:500
  253.4 1.2 collective-permute-start.5
  255.6 11.8 %all-to-all-done.2 = bf16[64,64,128]{2,1,0:T(8,128)(2,1)S(1)} async-done(((bf16[64,64,128]{2,1,0:T(8,128)(2,1)}), bf16[64,64,128]{2,1,0:T(8,128)(2,1)S(1)}, u32[]{:S(2)}, u32[]{:S(2)}) %all-to-all-start.2) | async-done | bytes 1048608 | tf_op jit(solution)/shard_map/all_to_all | solution.py:577
  267.6 2.6 collective-permute-start.6
  (66 shorter events, 13.7 us)
Async XLA Ops:
  7.2 3.0 %copy-start = (bf16[128,128]{1,0:T(8,128)(2,1)S(1)}, bf16[128,128]{1,0:T(8,128)(2,1)}, u32[]{:S(2)}) copy-start(bf16[128,128]{1,0:T(8,128)(2,1)} %param.12) | copy-start | bytes 98308
  7.2 85.2 %all-gather.3.cloned.1.call-start = ((), (), s32[]{:S(2)}) async-start(), calls=%async_computation.3 | async-start | bytes 9510912 | tf_op jit(solution)/shard_map/all_gather | solution.py:544
  11.5 35.8 %all-to-all-start = ((bf16[64,64,128]{2,1,0:T(8,128)(2,1)}), bf16[64,64,128]{2,1,0:T(8,128)(2,1)S(1)}, u32[]{:S(2)}, u32[]{:S(2)}) async-start(bf16[64,64,128]{2,1,0:T(8,128)(2,1)} %broadcast_in_dim.22), calls=%async_computation | async-start | bytes 2097152 | tf_op jit(solution)/shard_map/all_to_all | solution.py:504
  34.4 11.4 %copy-start.5 = (s32[128,4]{0,1:T(4,128)S(1)}, s32[128,4]{0,1:T(4,128)}, u32[]{:S(2)}) copy-start(s32[128,4]{0,1:T(4,128)} %param.13) | copy-start | bytes 6148
  34.4 19.4 %copy-start.4 = (bf16[128,32]{0,1:T(8,128)(2,1)S(1)}, bf16[128,32]{0,1:T(8,128)(2,1)}, u32[]{:S(2)}) copy-start(bf16[128,32]{0,1:T(8,128)(2,1)} %param.11) | copy-start | bytes 24580
  47.3 7.1 %collective-permute-start = (bf16[64,64,128]{2,1,0:T(8,128)(2,1)S(1)}, bf16[64,64,128]{2,1,0:T(8,128)(2,1)S(1)}, u32[]{:S(2)}, u32[]{:S(2)}) collective-permute-start(bf16[64,64,128]{2,1,0:T(8,128)(2,1)S(1)} %all-to-all-done), channel_id=1, source_target_pairs={{0,1},{1,0},{2,3},{3,2},{4,5},{5,4},{6,7},{7,6},{8,9},{9,8},{10,11... | collective-permute-start | bytes 3145736 | tf_op jit(solution)/shard_map/ppermute | solution.py:492
  92.4 63.3 %copy-start.2 = (f32[128,512]{1,0:T(8,128)S(1)}, f32[128,512]{1,0:T(8,128)}, u32[]{:S(2)}) copy-start(f32[128,512]{1,0:T(8,128)} %get-tuple-element.26) | copy-start | bytes 786436
  155.3 8.6 %collective-permute-start.2 = (bf16[64,288,128]{2,1,0:T(8,128)(2,1)}, bf16[64,288,128]{2,1,0:T(8,128)(2,1)S(1)}, u32[]{:S(2)}, u32[]{:S(2)}) collective-permute-start(bf16[64,288,128]{2,1,0:T(8,128)(2,1)} %get-tuple-element.30), channel_id=1, source_target_pairs={{0,1},{1,0},{2,3},{3,2},{4,5},{5,4},{6,7},{7,6},{8,9},{9,8},{10,11... | collective-permute-start | bytes 14155784 | tf_op jit(solution)/shard_map/ppermute | solution.py:492
  155.6 23.7 %collective-permute-start.1 = (f32[128,512]{1,0:T(8,128)S(1)}, f32[128,512]{1,0:T(8,128)S(1)}, u32[]{:S(2)}, u32[]{:S(2)}) collective-permute-start(f32[128,512]{1,0:T(8,128)S(1)} %copy-done.2), channel_id=1, source_target_pairs={{0,1},{1,0},{2,3},{3,2},{4,5},{5,4},{6,7},{7,6},{8,9},{9,8},{10,11... | collective-permute-start | bytes 786440 | tf_op jit(solution)/shard_map/ppermute | solution.py:492
  163.9 5.8 %copy-start.3 = (f32[128,512]{1,0:T(8,128)S(1)}, f32[128,512]{1,0:T(8,128)}, u32[]{:S(2)}) copy-start(f32[128,512]{1,0:T(8,128)} %get-tuple-element.31) | copy-start | bytes 786436
  169.7 10.4 %collective-permute-start.3 = (f32[128,512]{1,0:T(8,128)S(1)}, f32[128,512]{1,0:T(8,128)S(1)}, u32[]{:S(2)}, u32[]{:S(2)}) collective-permute-start(f32[128,512]{1,0:T(8,128)S(1)} %copy-done.3), channel_id=1, source_target_pairs={{0,1},{1,0},{2,3},{3,2},{4,5},{5,4},{6,7},{7,6},{8,9},{9,8},{10,11... | collective-permute-start | bytes 786440 | tf_op jit(solution)/shard_map/ppermute | solution.py:492
  169.9 71.1 %all-to-all-start.1 = ((bf16[64,288,128]{2,1,0:T(8,128)(2,1)}), bf16[64,288,128]{2,1,0:T(8,128)(2,1)}, u32[]{:S(2)}, u32[]{:S(2)}) async-start(bf16[64,288,128]{2,1,0:T(8,128)(2,1)} %add.89), calls=%async_computation.1 | async-start | bytes 9437184 | tf_op jit(solution)/shard_map/all_to_all | solution.py:563
  201.5 2.9 %collective-permute-start.4 = (bf16[64,64,128]{2,1,0:T(8,128)(2,1)S(1)}, bf16[64,64,128]{2,1,0:T(8,128)(2,1)S(1)}, u32[]{:S(2)}, u32[]{:S(2)}) collective-permute-start(bf16[64,64,128]{2,1,0:T(8,128)(2,1)S(1)} %dynamic-slice_bitcast_fusion), channel_id=1, source_target_pairs={{0,1},{1,0},{2,3},{3,2},{4,5},{5,4},{6,7},{7,6},{8,9},{9,8},{10,11... | collective-permute-start | bytes 3145736 | tf_op jit(solution)/shard_map/ppermute | solution.py:492
  227.9 43.8 %copy-start.1 = (bf16[128,128]{1,0:T(8,128)(2,1)S(1)}, bf16[128,128]{1,0:T(8,128)(2,1)}, u32[]{:S(2)}) copy-start(bf16[128,128]{1,0:T(8,128)(2,1)} %param.12) | copy-start | bytes 98308
  241.0 26.4 %all-to-all-start.2 = ((bf16[64,64,128]{2,1,0:T(8,128)(2,1)}), bf16[64,64,128]{2,1,0:T(8,128)(2,1)S(1)}, u32[]{:S(2)}, u32[]{:S(2)}) async-start(bf16[64,64,128]{2,1,0:T(8,128)(2,1)} %bitcast_add_fusion), calls=%async_computation.2 | async-start | bytes 2097152 | tf_op jit(solution)/shard_map/all_to_all | solution.py:577
  253.4 2.1 collective-permute-start.5
  267.6 3.5 %collective-permute-start.6 = (bf16[64,128]{1,0:T(8,128)(2,1)S(1)}, bf16[64,128]{1,0:T(8,128)(2,1)S(1)}, u32[]{:S(2)}, u32[]{:S(2)}) collective-permute-start(bf16[64,128]{1,0:T(8,128)(2,1)S(1)} %reduce_sum.95), channel_id=1, source_target_pairs={{0,1},{1,0},{2,3},{3,2},{4,5},{5,4},{6,7},{7,6},{8,9},{9,8},{10,11... | collective-permute-start | bytes 49160 | tf_op jit(solution)/shard_map/ppermute | solution.py:492
Sparse Core Ops, SparseCore 0:
  11.6 80.7 all-gather.2
